TPU v7x, 32 devices: a whole 2x2x4 slice. The times are simulated.
32 devices in a mesh: expert: 16 (over z, y, core), dp: 2 (over x).
Axes of the slice: x: 2, y: 2, z: 4, core: 2. Of those that a mesh axis runs over, the one named last changes fastest.
Arguments:
- tokens_in: bfloat16 [8192, 1024], P(('expert', 'dp')), may hold values from -6 to 6
- out_grad: bfloat16 [8192, 1024], P(('expert', 'dp')), may hold values from -4 to 4
- gates: bfloat16 [8192], P(('expert', 'dp')), may hold values from 0.19921875 to 1
- expert_ids: int32 [8192], P(('expert', 'dp')), may hold values from 0 to 7, as said below
- slot_ids: int32 [8192], P(('expert', 'dp')), may hold values from 0 to 35
- w_up: bfloat16 [16, 1024, 1024], P('expert'), may hold values from -0.1875 to 0.1875
- w_down: bfloat16 [16, 1024, 1024], P('expert'), may hold values from -0.125 to 0.125
Outputs:
- in_grad: bfloat16 [8192, 1024], P(('expert', 'dp'))
- gate_grad: bfloat16 [8192], P(('expert', 'dp'))
- up_grad: bfloat16 [16, 1024, 1024], P('expert', 'dp')
- down_grad: bfloat16 [16, 1024, 1024], P('expert', 'dp')
Inputs may be any that keep to these rules, and one draw needn't show every extreme that they name: `expert_ids`: the tokens of one device (aligned blocks of 256) take distinct pairs of expert and slot; no expert receives more than 36 tokens of one device, and one expert receives exactly 36 from every device.
All inputs are finite; a program needn't handle non-finite values.
Results may differ from a plain program's by a relative error of at most 0.015.
Values may be sent and summed in bfloat16 or wider, within the bound.
A program may use at most 64 MiB of HBM per device.

v0:
```python
import jax
import jax.numpy as jnp
from jax import lax
from jax.sharding import PartitionSpec as P


def gelu_parts(hidden):
    cdf = 0.5 * (1.0 + lax.erf(hidden * 0.7071067811865476))
    pdf = jnp.exp(-0.5 * hidden * hidden) * 0.3989422804014327
    return (hidden * cdf, cdf + hidden * pdf)


def packed(values, place, total):
    return jnp.zeros((total,) + values.shape[1:], values.dtype).at[place].set(values)


def on_device(tokens_in, out_grad, gates, expert_ids, slot_ids, w_up, w_down):
    devices_e = lax.axis_size("expert")
    rows = tokens_in.shape[0]
    width = tokens_in.shape[1]
    groups = devices_e // 2
    capacity = 9 * rows // (8 * groups)
    total = groups * capacity
    place = expert_ids * capacity + slot_ids
    up_w = w_up[0]
    down_w = w_down[0]
    gate_pack = packed(gates, place, total)
    gate_twice = jnp.broadcast_to(
        gate_pack.reshape(groups, 1, capacity), (groups, 2, capacity)
    ).reshape(devices_e * capacity)

    def doubled(values):
        return jnp.broadcast_to(
            values.reshape(groups, 1, capacity, width), (groups, 2, capacity, width)
        ).reshape(devices_e * capacity, width)

    x_slots, g_slots, gate_slots = (
        lax.all_to_all(
            doubled(packed(tokens_in, place, total)),
            "expert",
            split_axis=0,
            concat_axis=0,
            tiled=True,
        ),
        lax.all_to_all(
            doubled(packed(out_grad, place, total)),
            "expert",
            split_axis=0,
            concat_axis=0,
            tiled=True,
        ),
        lax.all_to_all(gate_twice, "expert", split_axis=0, concat_axis=0, tiled=True),
    )
    hidden = jnp.dot(x_slots, up_w, preferred_element_type=jnp.float32)
    value, slope = gelu_parts(hidden)
    expert_act = value.astype(jnp.bfloat16)
    expert_d_slots = (gate_slots.astype(jnp.float32)[:, None] * g_slots.astype(jnp.float32)).astype(
        jnp.bfloat16
    )
    out_part = jnp.dot(expert_act, down_w, preferred_element_type=jnp.float32).astype(jnp.bfloat16)
    gate_part = jnp.sum(g_slots.astype(jnp.float32) * out_part.astype(jnp.float32), axis=-1).astype(
        jnp.bfloat16
    )
    d_act = lax.dot_general(
        expert_d_slots, down_w, (((1,), (1,)), ((), ())), preferred_element_type=jnp.float32
    )
    expert_d_hidden = (d_act * slope).astype(jnp.bfloat16)
    d_part = lax.dot_general(
        expert_d_hidden, up_w, (((1,), (1,)), ((), ())), preferred_element_type=jnp.float32
    ).astype(jnp.bfloat16)
    act, d_slots, d_hidden, d_part, gate_part = (
        expert_act,
        expert_d_slots,
        expert_d_hidden,
        d_part,
        gate_part,
    )
    back_rows, back_gate = (
        lax.all_to_all(d_part, "expert", split_axis=0, concat_axis=0, tiled=True),
        lax.all_to_all(gate_part, "expert", split_axis=0, concat_axis=0, tiled=True),
    )
    row_sum = jnp.sum(
        back_rows.reshape(groups, 2, capacity, width).astype(jnp.float32), axis=1
    ).astype(jnp.bfloat16)
    gate_sum = jnp.sum(back_gate.reshape(groups, 2, capacity).astype(jnp.float32), axis=1).astype(
        jnp.bfloat16
    )
    in_grad = row_sum.reshape(total, width)[place]
    gate_grad = gate_sum.reshape(total)[place]
    piece = x_slots
    up_grad = lax.psum_scatter(
        lax.dot_general(
            piece, d_hidden, (((0,), (0,)), ((), ())), preferred_element_type=jnp.float32
        ).astype(jnp.bfloat16),
        "dp",
        scatter_dimension=0,
        tiled=True,
    )
    piece = act
    down_grad = lax.psum_scatter(
        lax.dot_general(
            piece, d_slots, (((0,), (0,)), ((), ())), preferred_element_type=jnp.float32
        ).astype(jnp.bfloat16),
        "dp",
        scatter_dimension=0,
        tiled=True,
    )
    return (in_grad, gate_grad, up_grad[None], down_grad[None])


def solution(mesh):
    return jax.shard_map(
        on_device,
        mesh=mesh,
        in_specs=(
            P(("expert", "dp"), None),
            P(("expert", "dp"), None),
            P(("expert", "dp")),
            P(("expert", "dp")),
            P(("expert", "dp")),
            P("expert", None, None),
            P("expert", None, None),
        ),
        out_specs=(
            P(("expert", "dp"), None),
            P(("expert", "dp")),
            P("expert", "dp", None),
            P("expert", "dp", None),
        ),
        check_vma=False,
    )
```

profile of v0, /device:TPU:0, one launch (start us, length us, event | category | flops | bytes accessed | tf_op | source)
XLA Modules:
  0.0 184.6 jit_solution(13285832223073832747)
XLA Ops:
  7.2 0.0 copy-start
  7.2 0.8 compare_select_fusion
  8.0 2.3 %scatter_custom_fusion = bf16[288]{0:T(512)(128)(2,1)S(1)} fusion(s32[256]{0:T(256)S(1)} %compare_select_fusion, bf16[256]{0:T(256)(128)(2,1)} %param.9, bf16[]{:T(256)} %constant.10.clone.1), kind=kCustom, calls=%fused_computation.37 | custom fusion | bytes 1088 | tf_op jit(solution)/shard_map/scatter | solution.py:14
  10.3 0.1 broadcast_in_dim.40
  10.4 0.6 copy.12
  11.0 7.4 %all-to-all-start = ((bf16[16,36,1]{1,2,0:T(2,128)(2,1)}), bf16[16,36,1]{1,2,0:T(2,128)(2,1)S(1)}, u32[]{:S(2)}, u32[]{:S(2)}) async-start(bf16[16,36,1]{1,2,0:T(2,128)(2,1)} %copy.12), calls=%async_computation | async-start | bytes 16384 | tf_op jit(solution)/shard_map/all_to_all | solution.py:52
  18.4 2.3 %scatter_custom_fusion.1 = bf16[288,1024]{1,0:T(8,128)(2,1)S(1)} fusion(s32[256]{0:T(256)S(1)} %compare_select_fusion, bf16[256,1024]{1,0:T(8,128)(2,1)} %param.8, bf16[]{:T(256)} %constant.10.clone.1), kind=kCustom, calls=%fused_computation.33 | custom fusion | bytes 590336 | tf_op jit(solution)/shard_map/scatter | solution.py:14
  20.8 0.1 broadcast_in_dim.42
  20.9 3.9 %all-to-all-done = bf16[16,36,1]{1,2,0:T(2,128)(2,1)S(1)} async-done(((bf16[16,36,1]{1,2,0:T(2,128)(2,1)}), bf16[16,36,1]{1,2,0:T(2,128)(2,1)S(1)}, u32[]{:S(2)}, u32[]{:S(2)}) %all-to-all-start) | async-done | bytes 1184 | tf_op jit(solution)/shard_map/all_to_all | solution.py:52
  24.8 1.2 broadcast_in_dim.43
  26.0 3.7 %all-to-all-start.1 = ((bf16[16,36,1024]{2,1,0:T(8,128)(2,1)}), bf16[16,36,1024]{2,1,0:T(8,128)(2,1)S(1)}, u32[]{:S(2)}, u32[]{:S(2)}) async-start(bf16[16,36,1024]{2,1,0:T(8,128)(2,1)} %bitcast.37), calls=%async_computation.1 | async-start | bytes 2621440 | tf_op jit(solution)/shard_map/all_to_all | solution.py:45
  29.7 3.0 %scatter_custom_fusion.2 = bf16[288,1024]{1,0:T(8,128)(2,1)} fusion(s32[256]{0:T(256)S(1)} %compare_select_fusion, bf16[256,1024]{1,0:T(8,128)(2,1)} %param.7, bf16[]{:T(256)} %constant.10.clone.1), kind=kCustom, calls=%fused_computation.31 | custom fusion | bytes 590336 | tf_op jit(solution)/shard_map/scatter | solution.py:14
  32.7 2.0 %broadcast_in_dim.44 = bf16[8,36,1024]{2,1,0:T(8,128)(2,1)} reshape(bf16[288,1024]{1,0:T(8,128)(2,1)} %scatter_custom_fusion.2) | data formatting | bytes 1179648 | tf_op jit(solution)/shard_map/broadcast_in_dim | solution.py:33
  34.7 22.3 %all-to-all-done.1 = bf16[16,36,1024]{2,1,0:T(8,128)(2,1)S(1)} async-done(((bf16[16,36,1024]{2,1,0:T(8,128)(2,1)}), bf16[16,36,1024]{2,1,0:T(8,128)(2,1)S(1)}, u32[]{:S(2)}, u32[]{:S(2)}) %all-to-all-start.1) | async-done | bytes 1179680 | tf_op jit(solution)/shard_map/all_to_all | solution.py:45
  57.0 2.3 %broadcast_in_dim.45 = bf16[8,2,36,1024]{3,2,1,0:T(8,128)(2,1)} broadcast(bf16[8,36,1024]{2,1,0:T(8,128)(2,1)} %broadcast_in_dim.44), dimensions={0,2,3} | broadcast | bytes 1769472 | tf_op jit(solution)/shard_map/broadcast_in_dim | solution.py:33
  59.4 8.0 %all-to-all-start.2 = ((bf16[16,36,1024]{2,1,0:T(8,128)(2,1)}), bf16[16,36,1024]{2,1,0:T(8,128)(2,1)}, u32[]{:S(2)}, u32[]{:S(2)}) async-start(bf16[16,36,1024]{2,1,0:T(8,128)(2,1)} %bitcast.36), calls=%async_computation.2 | async-start | bytes 2621440 | tf_op jit(solution)/shard_map/all_to_all | solution.py:38
  67.4 0.0 reduce-scatter.3.cloned.1.call-start
  67.5 1.4 multiply_convert_fusion
  68.9 2.2 %convert_element_type.76 = bf16[576,1024]{1,0:T(8,128)(2,1)} reshape(bf16[16,36,1024]{2,1,0:T(8,128)(2,1)} %multiply_convert_fusion) | data formatting | bytes 2359296 | tf_op jit(solution)/shard_map/convert_element_type | solution.py:57
  71.1 23.8 %all-to-all-done.2 = bf16[16,36,1024]{2,1,0:T(8,128)(2,1)} async-done(((bf16[16,36,1024]{2,1,0:T(8,128)(2,1)}), bf16[16,36,1024]{2,1,0:T(8,128)(2,1)}, u32[]{:S(2)}, u32[]{:S(2)}) %all-to-all-start.2) | async-done | bytes 1179680 | tf_op jit(solution)/shard_map/all_to_all | solution.py:38
  94.9 2.3 %all_to_all.36 = bf16[576,1024]{1,0:T(8,128)(2,1)} reshape(bf16[16,36,1024]{2,1,0:T(8,128)(2,1)} %all-to-all-done.2) | data formatting | bytes 2359296 | tf_op jit(solution)/shard_map/all_to_all | solution.py:38
  97.1 0.0 copy-done
  97.2 4.0 %multiply_convert_fusion.2 = (bf16[576,1024]{1,0:T(8,128)(2,1)}, f32[576,1024]{1,0:T(8,128)S(1)}) fusion(bf16[576,1024]{1,0:T(8,128)(2,1)} %all_to_all.36, bf16[1,1024,1024]{2,1,0:T(8,128)(2,1)S(1)} %copy-done), kind=kOutput, calls=%fused_computation.15 | convolution fusion | flops 1210908672 | bytes 6815744 | tf_op jit(solution)/shard_map/dot_general | solution.py:54
  101.1 0.0 copy-done.1
  101.2 2.2 %fusion.5 = bf16[576,1024]{1,0:T(8,128)(2,1)S(1)} fusion(f32[576,1024]{1,0:T(8,128)S(1)} %get-tuple-element.5, bf16[576,1024]{1,0:T(8,128)(2,1)S(1)} %copy-done.1, bf16[1,1024,1024]{2,1,0:T(8,128)(2,1)S(1)} %copy-done.3), kind=kOutput, calls=%fused_computation.12 | convolution fusion | flops 1213857792 | bytes 6815744 | tf_op jit(solution)/shard_map/dot_general | solution.py:64
  103.4 1.1 copy-done.5
  104.5 3.2 %convolution_convert_fusion.1 = bf16[1024,1024]{1,0:T(8,128)(2,1)} fusion(bf16[576,1024]{1,0:T(8,128)(2,1)S(1)} %copy-done.2, bf16[576,1024]{1,0:T(8,128)(2,1)S(1)} %fusion.5), kind=kOutput, calls=%fused_computation.26 | convolution fusion | flops 1209008128 | bytes 4456448 | tf_op jit(solution)/shard_map/dot_general | solution.py:92
  107.6 0.0 reduce-scatter.3.cloned.1.call-update
  107.7 0.2 reduce-scatter.5.cloned.1.call-start
  107.9 0.1 reshape.79
  108.0 1.5 reshape.78
  109.5 5.3 %convolution_convert_fusion = bf16[1024,1024]{1,0:T(8,128)(2,1)} fusion(bf16[576,1024]{1,0:T(8,128)(2,1)} %get-tuple-element.4, f32[576,1024]{1,0:T(8,128)} %reshape.78, f32[576]{0:T(1024)S(1)} %reshape.79), kind=kOutput, calls=%fused_computation.25 | convolution fusion | flops 1210187776 | bytes 5638400 | tf_op jit(solution)/shard_map/dot_general | solution.py:101
  114.8 0.0 reduce-scatter.5.cloned.1.call-update
  114.8 1.2 copy-done.4
  116.1 4.5 %multiply_reduce_fusion = bf16[576]{0:T(1024)(128)(2,1)S(1)} fusion(f32[576,1024]{1,0:T(8,128)} %reshape.78, bf16[576,1024]{1,0:T(8,128)(2,1)S(1)} %copy-done.4, bf16[1,1024,1024]{2,1,0:T(8,128)(2,1)} %param.13), kind=kOutput, calls=%fused_computation.14 | convolution fusion | flops 1210318336 | bytes 5637248 | tf_op jit(solution)/shard_map/dot_general | solution.py:60
  120.5 0.7 convert_element_type.94
  121.3 7.6 %all-to-all-start.4 = ((bf16[16,36,1]{1,2,0:T(2,128)(2,1)}), bf16[16,36,1]{1,2,0:T(2,128)(2,1)S(1)}, u32[]{:S(2)}, u32[]{:S(2)}) async-start(bf16[16,36,1]{1,2,0:T(2,128)(2,1)} %convert_element_type.94), calls=%async_computation.4 | async-start | bytes 16384 | tf_op jit(solution)/shard_map/all_to_all | solution.py:80
  128.8 2.7 %fusion.17 = bf16[576,1024]{1,0:T(8,128)(2,1)S(1)} fusion(bf16[576,1024]{1,0:T(8,128)(2,1)} %copy-done.5, bf16[1,1024,1024]{2,1,0:T(8,128)(2,1)S(1)} %copy-done), kind=kOutput, calls=%fused_computation.28 | convolution fusion | flops 1208549376 | bytes 4456448 | tf_op jit(solution)/shard_map/dot_general | solution.py:68
  131.5 1.2 all_to_all.37
  132.7 2.4 %all-to-all-done.4 = bf16[16,36,1]{1,2,0:T(2,128)(2,1)S(1)} async-done(((bf16[16,36,1]{1,2,0:T(2,128)(2,1)}), bf16[16,36,1]{1,2,0:T(2,128)(2,1)S(1)}, u32[]{:S(2)}, u32[]{:S(2)}) %all-to-all-start.4) | async-done | bytes 1184 | tf_op jit(solution)/shard_map/all_to_all | solution.py:80
  135.2 3.7 %all-to-all-start.3 = ((bf16[16,36,1024]{2,1,0:T(8,128)(2,1)}), bf16[16,36,1024]{2,1,0:T(8,128)(2,1)S(1)}, u32[]{:S(2)}, u32[]{:S(2)}) async-start(bf16[16,36,1024]{2,1,0:T(8,128)(2,1)} %all_to_all.37), calls=%async_computation.3 | async-start | bytes 2621440 | tf_op jit(solution)/shard_map/all_to_all | solution.py:79
  138.9 0.1 reshape.76
  139.0 2.5 %gather_fusion.1 = bf16[256]{0:T(256)(128)(2,1)} fusion(bf16[288]{0:T(512)(128)(2,1)S(1)} %reshape.76, s32[1024]{0:T(1024)S(1)} %pad_clamp_fusion), kind=kCustom, calls=%fused_computation.1 | custom fusion | bytes 2048 | tf_op jit(solution)/shard_map/gather | solution.py:89
  141.5 24.8 %all-to-all-done.3 = bf16[16,36,1024]{2,1,0:T(8,128)(2,1)S(1)} async-done(((bf16[16,36,1024]{2,1,0:T(8,128)(2,1)}), bf16[16,36,1024]{2,1,0:T(8,128)(2,1)S(1)}, u32[]{:S(2)}, u32[]{:S(2)}) %all-to-all-start.3) | async-done | bytes 1179680 | tf_op jit(solution)/shard_map/all_to_all | solution.py:79
  166.2 1.2 bitcast_reduce_fusion
  167.4 1.2 reshape.74
  168.6 2.0 %gather_fusion = bf16[256,1024]{1,0:T(8,128)(2,1)} fusion(bf16[288,1024]{1,0:T(8,128)(2,1)S(1)} %reshape.74, s32[1024]{0:T(1024)S(1)} %pad_clamp_fusion), kind=kCustom, calls=%fused_computation | custom fusion | bytes 1049600 | tf_op jit(solution)/shard_map/gather | solution.py:88
  170.6 7.2 %reduce-scatter.5.cloned.1.call-done = bf16[512,1024]{1,0:T(8,128)(2,1)} async-done(((bf16[1024,1024]{1,0:T(8,128)(2,1)}), bf16[512,1024]{1,0:T(8,128)(2,1)}) %reduce-scatter.5.cloned.1.call-update) | async-done | bytes 1048592 | tf_op jit(solution)/shard_map/reduce_scatter | solution.py:100
  (14 shorter events, 0.1 us)
Async XLA Ops:
  7.2 90.0 %copy-start = (bf16[1,1024,1024]{2,1,0:T(8,128)(2,1)S(1)}, bf16[1,1024,1024]{2,1,0:T(8,128)(2,1)}, u32[]{:S(2)}) copy-start(bf16[1,1024,1024]{2,1,0:T(8,128)(2,1)} %param.12) | copy-start | bytes 6291460
  11.0 13.7 %all-to-all-start = ((bf16[16,36,1]{1,2,0:T(2,128)(2,1)}), bf16[16,36,1]{1,2,0:T(2,128)(2,1)S(1)}, u32[]{:S(2)}, u32[]{:S(2)}) async-start(bf16[16,36,1]{1,2,0:T(2,128)(2,1)} %copy.12), calls=%async_computation | async-start | bytes 16384 | tf_op jit(solution)/shard_map/all_to_all | solution.py:52
  26.0 31.1 %all-to-all-start.1 = ((bf16[16,36,1024]{2,1,0:T(8,128)(2,1)}), bf16[16,36,1024]{2,1,0:T(8,128)(2,1)S(1)}, u32[]{:S(2)}, u32[]{:S(2)}) async-start(bf16[16,36,1024]{2,1,0:T(8,128)(2,1)} %bitcast.37), calls=%async_computation.1 | async-start | bytes 2621440 | tf_op jit(solution)/shard_map/all_to_all | solution.py:45
  59.4 35.5 %all-to-all-start.2 = ((bf16[16,36,1024]{2,1,0:T(8,128)(2,1)}), bf16[16,36,1024]{2,1,0:T(8,128)(2,1)}, u32[]{:S(2)}, u32[]{:S(2)}) async-start(bf16[16,36,1024]{2,1,0:T(8,128)(2,1)} %bitcast.36), calls=%async_computation.2 | async-start | bytes 2621440 | tf_op jit(solution)/shard_map/all_to_all | solution.py:38
  67.4 103.2 %reduce-scatter.3.cloned.1.call-start = ((), (), s32[]{:S(2)}) async-start(), calls=%async_computation.7 | async-start | bytes 3145728 | tf_op jit(solution)/shard_map/reduce_scatter | solution.py:91
  97.2 4.0 %copy-start.1 = (bf16[576,1024]{1,0:T(8,128)(2,1)S(1)}, bf16[576,1024]{1,0:T(8,128)(2,1)}, u32[]{:S(2)}) copy-start(bf16[576,1024]{1,0:T(8,128)(2,1)} %convert_element_type.76) | copy-start | bytes 3538948
  97.2 4.0 %copy-start.3 = (bf16[1,1024,1024]{2,1,0:T(8,128)(2,1)S(1)}, bf16[1,1024,1024]{2,1,0:T(8,128)(2,1)}, u32[]{:S(2)}) copy-start(bf16[1,1024,1024]{2,1,0:T(8,128)(2,1)} %param.13) | copy-start | bytes 6291460
  101.2 3.3 %copy-start.2 = (bf16[576,1024]{1,0:T(8,128)(2,1)S(1)}, bf16[576,1024]{1,0:T(8,128)(2,1)}, u32[]{:S(2)}) copy-start(bf16[576,1024]{1,0:T(8,128)(2,1)} %all_to_all.36) | copy-start | bytes 3538948
  103.3 1.1 copy-start.5
  107.7 70.1 %reduce-scatter.5.cloned.1.call-start = ((), (), s32[]{:S(2)}) async-start(), calls=%async_computation.8 | async-start | bytes 3145728 | tf_op jit(solution)/shard_map/reduce_scatter | solution.py:100
  114.8 1.3 copy-start.4
  121.3 13.9 %all-to-all-start.4 = ((bf16[16,36,1]{1,2,0:T(2,128)(2,1)}), bf16[16,36,1]{1,2,0:T(2,128)(2,1)S(1)}, u32[]{:S(2)}, u32[]{:S(2)}) async-start(bf16[16,36,1]{1,2,0:T(2,128)(2,1)} %convert_element_type.94), calls=%async_computation.4 | async-start | bytes 16384 | tf_op jit(solution)/shard_map/all_to_all | solution.py:80
  135.2 31.1 %all-to-all-start.3 = ((bf16[16,36,1024]{2,1,0:T(8,128)(2,1)}), bf16[16,36,1024]{2,1,0:T(8,128)(2,1)S(1)}, u32[]{:S(2)}, u32[]{:S(2)}) async-start(bf16[16,36,1024]{2,1,0:T(8,128)(2,1)} %all_to_all.37), calls=%async_computation.3 | async-start | bytes 2621440 | tf_op jit(solution)/shard_map/all_to_all | solution.py:79
Sparse Core Ops, SparseCore 0:
  107.8 35.1 reduce-scatter.2
  145.9 31.8 reduce-scatter.4
where the time goes:
time: 185 us
  waiting for transfers between devices  84.4 us (46%)
  starting transfers between devices  30.7 us (17%)
  local copies, waits for them, and re-layouts  30.1 us (16%)
  matrix products  21.8 us (12%)
  between operations  14.2 us (8%)
  other arithmetic  3.46 us (2%)
    all_to_all x1, waiting for transfers between devices, on_device(): lax.all_to_all(d_part, 'expert', split_axis=0, concat_axis=0, tiled=True)  24.8 us
    all_to_all x1, waiting for transfers between devices, on_device(): lax.all_to_all(doubled(packed(tokens_in, place, total)), 'expert', split_...  23.8 us
    all_to_all x1, waiting for transfers between devices, on_device(): lax.all_to_all(doubled(packed(out_grad, place, total)), 'expert', split_a...  22.3 us
    all_to_all x1, starting transfers between devices, on_device(): lax.all_to_all(doubled(packed(tokens_in, place, total)), 'expert', split_...  8.03 us
    scatter x3, local copies, waits for them, and re-layouts, packed(): jnp.zeros((total,) + values.shape[1:], values.dtype).at[place].set(values)  7.61 us
    all_to_all x1, starting transfers between devices, on_device(): lax.all_to_all(gate_part, 'expert', split_axis=0, concat_axis=0, tiled=True)  7.57 us
    all_to_all x1, starting transfers between devices, on_device(): lax.all_to_all(gate_twice, 'expert', split_axis=0, concat_axis=0, tiled=T...  7.39 us
    reduce_scatter x1, waiting for transfers between devices, on_device(): lax.psum_scatter(lax.dot_general(piece, d_slots, (((0,), (0,)), ((), ()))...  7.17 us
  transfers between devices with their start and end apart: 7, of which 6 were waited for; matrix products, arithmetic and copies ran while one was open for 18% of the time, Pallas kernels for 0%

commit v1 on v0

v1 whole, which is shorter than its diff:
```python
import functools

import jax
import jax.numpy as jnp
from jax import lax
from jax.experimental import pallas as pl
from jax.experimental.pallas import tpu as pltpu
from jax.sharding import PartitionSpec as P

F32 = jnp.float32
BF16 = jnp.bfloat16


def xor(a, b, count):
    total, bit = 0, 1
    while bit < count:
        total = total + lax.rem(a // bit + b // bit, 2) * bit
        bit *= 2
    return total


def gelu_parts(hidden):
    cdf = 0.5 * (1.0 + lax.erf(hidden * 0.7071067811865476))
    pdf = jnp.exp(-0.5 * hidden * hidden) * 0.3989422804014327
    return (hidden * cdf, cdf + hidden * pdf)


def dot(a, b, da, db):
    return lax.dot_general(a, b, (((da,), (db,)), ((), ())), preferred_element_type=F32)


def kernel(
    chips, dps, cap, rows,
    place_ref, gates_ref, tok_ref, cot_ref, up_hbm, down_hbm,
    in_ref, gate_ref, upg_ref, downg_ref,
    tx, rx, xc, dc, actc, dhc, part, sib, xr, fin, wu, wd, ugs, ugr,
    w_sem, ici_s, ici_r, sf_s, sf_r, xf_s, xf_r, ps_s, ps_r, xr_s, xr_r, fin_s, fin_r, ug_s, ug_r,
):
    me = lax.axis_index("expert")
    k = lax.axis_index("dp")
    g = me // 2
    c = lax.rem(me, 2)
    o = 1 - c
    width = tok_ref.shape[1]
    half = width // 2
    hq = wu.shape[1]
    dblk = width // dps
    per = 2 * dps * rows

    def dev(chip, core, dp):
        return {"expert": chip * 2 + core, "dp": dp}

    def other(j):
        return lax.rem(k + j, dps)

    def remote(src, dst, s, r, target):
        return pltpu.make_async_remote_copy(
            src_ref=src, dst_ref=dst, send_sem=s, recv_sem=r,
            device_id=target, device_id_type=pl.DeviceIdType.MESH,
        )

    def ici(i):
        return remote(tx.at[i], rx.at[i, c, k], ici_s.at[i], ici_r.at[i], dev(xor(g, i, chips), c, k))

    def side(i, core, kk):
        return remote(
            rx.at[i, core, kk], rx.at[i, core, kk], sf_s.at[i, kk], sf_r.at[i, kk], dev(g, o, k)
        )

    def cross(i, kk, slot):
        return remote(
            rx.at[i, c, slot], rx.at[i, c, slot], xf_s.at[i, kk], xf_r.at[i, slot], dev(g, c, kk)
        )

    def half_sum(i, kk):
        return remote(part.at[i, o, kk], sib.at[i, kk], ps_s.at[i, kk], ps_r.at[i, kk], dev(g, o, k))

    def cross_sum(i, kk, slot):
        return remote(
            part.at[i, c, kk], xr.at[i, slot], xr_s.at[i, kk], xr_r.at[i, slot], dev(g, c, kk)
        )

    def home(i):
        return remote(part.at[i, c, k], fin.at[i], fin_s.at[i], fin_r.at[i], dev(xor(g, i, chips), c, k))

    tile = min(256, dblk)
    tiles = dblk // tile

    def up_send(j, m, kk, slot):
        return remote(
            ugs.at[j - 1, pl.ds(m * tile, tile)], ugr.at[slot, pl.ds(m * tile, tile)],
            ug_s.at[kk, m], ug_r.at[slot, m], dev(g, c, kk),
        )

    load_up = pltpu.make_async_copy(
        up_hbm.at[0, :, pl.ds(pl.multiple_of(k * hq, hq), hq)], wu, w_sem.at[0]
    )
    load_down = pltpu.make_async_copy(
        down_hbm.at[0, pl.ds(pl.multiple_of(k * hq, hq), hq), :], wd, w_sem.at[1]
    )
    load_up.start()
    load_down.start()

    barrier = pltpu.get_barrier_semaphore()

    def greet(target):
        pl.semaphore_signal(barrier, inc=1, device_id=target, device_id_type=pl.DeviceIdType.MESH)

    @pl.loop(1, chips)
    def _(i):
        greet(dev(xor(g, i, chips), c, k))

    greet(dev(g, o, k))
    for j in range(1, dps):
        greet(dev(g, c, other(j)))

    eye = lax.broadcasted_iota(jnp.int32, (1, rows, 128), 1) == lax.broadcasted_iota(
        jnp.int32, (1, rows, 128), 2
    )
    at_cap = lax.broadcasted_iota(jnp.int32, (1, rows, 128), 1) == cap

    def one_hot():
        slots = lax.broadcasted_iota(jnp.int32, (chips * rows, tok_ref.shape[0]), 0)
        return slots == place_ref[...]

    hot = one_hot()
    hot16 = jnp.where(hot, 1.0, 0.0).astype(BF16)
    gate_col = jnp.sum(jnp.where(hot, gates_ref[...].astype(F32), 0.0), axis=1, keepdims=True)
    gate_row = jnp.sum(jnp.where(eye, gate_col.reshape(chips, rows, 1), 0.0), axis=1, keepdims=True)
    x_pack = dot(hot16, tok_ref[...], 1, 0).reshape(chips, rows, width)
    g_pack = dot(hot16, cot_ref[...], 1, 0).reshape(chips, rows, width)
    first = jnp.where(at_cap, gate_row, x_pack[:, :, :128])
    x_pack = jnp.concatenate([first, x_pack[:, :, 128:]], axis=2)
    both = jnp.concatenate([x_pack, g_pack], axis=1).astype(BF16)
    tx[...] = both
    rx[0, c, k] = both[0]

    pl.semaphore_wait(barrier, chips - 1 + 1 + dps - 1)

    @pl.loop(1, chips)
    def _(i):
        ici(i).start()

    def stage_a(i):
        @pl.when(i > 0)
        def _():
            ici(i).wait_recv()

        for j in range(1, dps):
            cross(i, other(j), k).start()
        side(i, c, k).start()

    def stage_b(i):
        for j in range(1, dps):
            cross(i, other(j), other(j)).wait_recv()
            side(i, c, other(j)).start()

    def stage_c(i):
        for kk in range(dps):
            side(i, o, kk).wait_recv()
        blk = rx[i].reshape(2 * dps, 2 * rows, width).astype(F32)
        x = blk[:, :rows].reshape(per, width).astype(BF16)
        cot = blk[:, rows:].reshape(per, width)
        gate = jnp.sum(
            jnp.where(eye, blk[:, cap : cap + 1, :128], 0.0), axis=2, keepdims=True
        ).reshape(per, 1)
        at = pl.ds(pl.multiple_of(i * per, per), per)
        xc[at, :] = x
        dc[at, :] = (gate * cot).astype(BF16)
        hidden = dot(x, wu[...], 1, 0)
        gv = dot(cot.astype(BF16), wd[...], 1, 1)
        value, slope = gelu_parts(hidden)
        act = value.astype(BF16)
        dh = (gate * gv * slope).astype(BF16)
        actc[at, :] = act
        dhc[at, :] = dh
        gp = jnp.sum(act.astype(F32) * gv, axis=1, keepdims=True).reshape(2 * dps, rows, 1)
        gp_row = jnp.sum(jnp.where(eye, gp, 0.0), axis=1, keepdims=True)
        d = dot(dh, wu[...], 1, 1).reshape(2 * dps, rows, width)
        lead = jnp.where(at_cap, gp_row, d[:, :, :128])
        left = jnp.concatenate([lead, d[:, :, 128:half]], axis=2)
        whole = jnp.concatenate([left, d[:, :, half:]], axis=1).astype(BF16)
        part[i] = whole.reshape(2, dps, 2 * rows, half)
        for kk in range(dps):
            half_sum(i, kk).start()

    def stage_d(i):
        for j in list(range(1, dps)) + [0]:
            kk = other(j)
            half_sum(i, kk).wait_recv()
            part[i, c, kk] = (part[i, c, kk].astype(F32) + sib[i, kk].astype(F32)).astype(BF16)
            if j:
                cross_sum(i, kk, dps - 1 - j).start()

    def stage_e(i):
        total = part[i, c, k].astype(F32)
        for j in range(1, dps):
            cross_sum(i, other(j), j - 1).wait_recv()
            total = total + xr[i, j - 1].astype(F32)
        total = total.astype(BF16)

        @pl.when(i > 0)
        def _():
            part[i, c, k] = total
            home(i).start()

        @pl.when(i == 0)
        def _():
            fin[0] = total

    load_up.wait()
    load_down.wait()

    @pl.loop(0, chips + 2)
    def _(t):
        @pl.when(t < chips)
        def _():
            stage_a(t)

        @pl.when(jnp.logical_and(t >= 1, t < chips + 1))
        def _():
            stage_b(t - 1)

        @pl.when(t >= 2)
        def _():
            stage_c(t - 2)

        @pl.when(t >= 3)
        def _():
            stage_d(t - 3)

        @pl.when(t >= 4)
        def _():
            stage_e(t - 4)

    stage_d(chips - 1)

    def up_tile(kk, m):
        at = pl.ds(pl.multiple_of(kk * dblk + m * tile, tile), tile)
        return dot(xc[:, at], dhc[...], 0, 0).astype(BF16)

    for j in range(1, dps):
        @pl.loop(0, tiles)
        def _(m):
            ugs[j - 1, pl.ds(pl.multiple_of(m * tile, tile), tile), :] = up_tile(other(j), m)
            up_send(j, m, other(j), dps - 1 - j).start()

    stage_e(chips - 2)
    stage_e(chips - 1)
    mine = pl.ds(pl.multiple_of(k * hq, hq), hq)

    @pl.loop(0, tiles)
    def _(m):
        upg_ref[pl.ds(pl.multiple_of(m * tile, tile), tile), mine] = up_tile(k, m)

    dtile = min(256, hq)

    @pl.loop(0, hq // dtile)
    def _(m):
        at = pl.ds(pl.multiple_of(m * dtile, dtile), dtile)
        downg_ref[at, :] = dot(actc[:, at], dc[...], 0, 0).astype(BF16)

    @pl.loop(1, chips)
    def _(i):
        home(i).wait_recv()

    hot = one_hot()
    hot16 = jnp.where(hot, 1.0, 0.0).astype(BF16)
    back = fin[...].astype(F32)
    left = back[:, :rows].reshape(chips * rows, half).astype(BF16)
    right = back[:, rows:].reshape(chips * rows, half).astype(BF16)
    in_ref[:, :half] = dot(hot16, left, 0, 0).astype(BF16)
    in_ref[:, half:] = dot(hot16, right, 0, 0).astype(BF16)
    col = jnp.sum(
        jnp.where(eye, back[:, cap : cap + 1, :128], 0.0), axis=2, keepdims=True
    ).reshape(chips * rows, 1)
    gate_ref[...] = jnp.sum(jnp.where(hot, col, 0.0), axis=0, keepdims=True).astype(BF16)

    for j in range(1, dps):
        kk = other(j)

        @pl.loop(0, tiles)
        def _(m):
            up_send(j, m, kk, j - 1).wait_recv()

        upg_ref[:, pl.ds(pl.multiple_of(kk * hq, hq), hq)] = ugr[j - 1]

    @pl.loop(0, chips)
    def _(i):
        @pl.when(i > 0)
        def _():
            ici(i).wait_send()
            home(i).wait_send()

        for kk in range(dps):
            side(i, c, kk).wait_send()
            half_sum(i, kk).wait_send()
        for j in range(1, dps):
            cross(i, other(j), k).wait_send()
            cross_sum(i, other(j), dps - 1 - j).wait_send()

    for j in range(1, dps):
        @pl.loop(0, tiles)
        def _(m):
            up_send(j, m, other(j), dps - 1 - j).wait_send()


def on_device(tokens_in, out_grad, gates, expert_ids, slot_ids, w_up, w_down):
    chips = lax.axis_size("expert") // 2
    dps = lax.axis_size("dp")
    tokens, width = tokens_in.shape
    hidden = w_up.shape[2]
    cap = 9 * tokens // (8 * chips)
    rows = (cap + 1 + 7) // 8 * 8
    hq = hidden // dps
    dblk = width // dps
    g = lax.axis_index("expert") // 2
    place = (jnp.bitwise_xor(expert_ids, g) * rows + slot_ids).reshape(1, tokens)
    slots = 2 * dps * chips * rows
    tiles = dblk // min(256, dblk)
    vmem = pl.BlockSpec(memory_space=pltpu.VMEM)
    hbm = pl.BlockSpec(memory_space=pl.ANY)
    dma = pltpu.SemaphoreType.DMA
    in_grad, gate_grad, up_grad, down_grad = pl.pallas_call(
        functools.partial(kernel, chips, dps, cap, rows),
        out_shape=(
            jax.ShapeDtypeStruct((tokens, width), BF16),
            jax.ShapeDtypeStruct((1, tokens), BF16),
            jax.ShapeDtypeStruct((dblk, hidden), BF16),
            jax.ShapeDtypeStruct((hq, width), BF16),
        ),
        in_specs=[vmem] * 4 + [hbm] * 2,
        out_specs=(vmem,) * 4,
        scratch_shapes=[
            pltpu.VMEM((chips, 2 * rows, width), BF16),
            pltpu.VMEM((chips, 2, dps, 2 * rows, width), BF16),
            pltpu.VMEM((slots, width), BF16),
            pltpu.VMEM((slots, width), BF16),
            pltpu.VMEM((slots, hq), BF16),
            pltpu.VMEM((slots, hq), BF16),
            pltpu.VMEM((chips, 2, dps, 2 * rows, width // 2), BF16),
            pltpu.VMEM((chips, dps, 2 * rows, width // 2), BF16),
            pltpu.VMEM((chips, dps - 1, 2 * rows, width // 2), BF16),
            pltpu.VMEM((chips, 2 * rows, width // 2), BF16),
            pltpu.VMEM((width, hq), BF16),
            pltpu.VMEM((hq, width), BF16),
            pltpu.VMEM((dps - 1, dblk, hq), BF16),
            pltpu.VMEM((dps - 1, dblk, hq), BF16),
            dma((2,)),
            dma((chips,)),
            dma((chips,)),
            dma((chips, dps)),
            dma((chips, dps)),
            dma((chips, dps)),
            dma((chips, dps)),
            dma((chips, dps)),
            dma((chips, dps)),
            dma((chips, dps)),
            dma((chips, dps)),
            dma((chips,)),
            dma((chips,)),
            dma((dps, tiles)),
            dma((dps, tiles)),
        ],
        compiler_params=pltpu.CompilerParams(
            collective_id=0, has_side_effects=True, vmem_limit_bytes=61 * 1024 * 1024
        ),
    )(place, gates.reshape(1, tokens), tokens_in, out_grad, w_up, w_down)
    return (in_grad, gate_grad.reshape(tokens), up_grad[None], down_grad[None])


def solution(mesh):
    return jax.shard_map(
        on_device,
        mesh=mesh,
        in_specs=(
            P(("expert", "dp"), None),
            P(("expert", "dp"), None),
            P(("expert", "dp")),
            P(("expert", "dp")),
            P(("expert", "dp")),
            P("expert", None, None),
            P("expert", None, None),
        ),
        out_specs=(
            P(("expert", "dp"), None),
            P(("expert", "dp")),
            P("expert", "dp", None),
            P("expert", "dp", None),
        ),
        check_vma=False,
    )
```

time: 185 us -> 81.6 us (0.44)
  waiting for transfers between devices: 84.4 us -> 0 us
  Pallas kernels: 0 us -> 71.8 us
  starting transfers between devices: 30.7 us -> 0 us
  local copies, waits for them, and re-layouts: 30.1 us -> 6.32 us
  matrix products: 21.8 us -> 0 us
  between operations: 14.2 us -> 0.66 us
    all_to_all x5 -> x0, waiting for transfers between devices: 77.2 us -> none  [the longest x1 24.8 us: on_device(): lax.all_to_all(d_part, 'expert', split_axis=0, concat_axis=0, tiled=True)]
    pallas_call x0 -> x1, Pallas kernels: none -> 71.8 us  [on_device(): pl.pallas_call(functools.partial(kernel, chips, dps, cap, rows), out_shap...]
    all_to_all x5 -> x0, starting transfers between devices: 30.4 us -> none  [the longest x1 8.03 us: on_device(): lax.all_to_all(doubled(packed(tokens_in, place, total)), 'expert', split_...]
    dot_general x6 -> x0, matrix products: 21.8 us -> none  [the longest x1 5.26 us: on_device(): lax.dot_general(piece, d_slots, (((0,), (0,)), ((), ())), preferred_eleme...]
    scatter x3 -> x0, local copies, waits for them, and re-layouts: 7.61 us -> none  [packed(): jnp.zeros((total,) + values.shape[1:], values.dtype).at[place].set(values)]
    reduce_scatter x2 -> x0, waiting for transfers between devices: 7.17 us -> none  [the longest x1 7.17 us: on_device(): lax.psum_scatter(lax.dot_general(piece, d_slots, (((0,), (0,)), ((), ()))...]
    broadcast_in_dim x6 -> x0, local copies, waits for them, and re-layouts: 5.79 us -> none  [the longest x4 5.69 us: doubled(): jnp.broadcast_to(values.reshape(groups, 1, capacity, width), (groups, 2,...]
    convert_element_type x4 -> x0, local copies, waits for them, and re-layouts: 4.56 us -> none  [the longest x1 2.24 us: on_device(): (gate_slots.astype(jnp.float32)[:, None] * g_slots.astype(jnp.float32)).a...]
  transfers between devices with their start and end apart: 7 -> 0, of which waited for: 6 -> 0; matrix products, arithmetic and copies ran while one was open for 18% -> 0% of each run, Pallas kernels for 0% -> 0%
where the time goes in v1:
time: 81.6 us; the launch traced here: 81.3 us
  Pallas kernels  71.8 us (88%)
  local copies, waits for them, and re-layouts  6.32 us (8%)
  other arithmetic  2.55 us (3%)
    pallas_call x1, Pallas kernels, on_device(): pl.pallas_call(functools.partial(kernel, chips, dps, cap, rows), out_shap...  71.8 us
    unnamed x5, local copies, waits for them, and re-layouts  5.1 us

profile of v1, /device:TPU:0, one launch (start us, length us, event | category | flops | bytes accessed | tf_op | source)
XLA Modules:
  0.0 81.3 jit_solution(15226708365653383420)
XLA Ops:
  0.6 1.3 %multiply_add_fusion = s32[256]{0:T(256)} fusion(s32[256]{0:T(256)} %param.11, s32[256]{0:T(256)} %param.10, s32[]{:T(128)S(6)} %select_n.5), kind=kLoop, calls=%fused_computation | loop fusion | flops 768 | bytes 3076 | tf_op jit(solution)/shard_map/add | solution.py:318
  1.9 1.2 %reshape.18.gates_ref = bf16[1,256]{1,0:T(2,128)(2,1)} reshape(bf16[256]{0:T(256)(128)(2,1)} %param.9) | data formatting | bytes 1024 | tf_op jit(solution)/shard_map/reshape | solution.py:368
  3.1 71.8 %shard_map.102 = (bf16[256,1024]{1,0:T(8,128)(2,1)}, bf16[1,256]{1,0:T(2,128)(2,1)}, bf16[512,1024]{1,0:T(8,128)(2,1)}, bf16[512,1024]{1,0:T(8,128)(2,1)}) custom-call(s32[1,256]{1,0:T(1,128)} %bitcast.5, bf16[1,256]{1,0:T(2,128)(2,1)} %reshape.18.gates_ref, bf16[256,1024]{1,0:T(8,128)(2,1)} %tok_ref.1, bf16[256,1024]{1,0:T(8,128)(2,1)} %cot_ref.1, ...), custom_call_target="tpu_custom_call" | custom-call | tf_op jit(solution)/shard_map/pallas_call | solution.py:324
  74.9 0.0 copy-start
  74.9 1.3 %reduce = bf16[256]{0:T(256)(128)(2,1)} reduce(bf16[1,256]{1,0:T(2,128)(2,1)} %get-tuple-element.9, bf16[]{:T(256)} %constant.24), dimensions={0}, to_apply=%get-tuple-element.9.reduce_sub_computation | reduce | bytes 1026 | tf_op jit(solution)/shard_map/pallas_call | solution.py:324
  76.2 1.9 %copy.14 = bf16[256,1024]{1,0:T(8,128)(2,1)} copy(bf16[256,1024]{1,0:T(8,128)(2,1)} %get-tuple-element.16) | data formatting | bytes 1048576
  78.1 2.3 %copy.15 = bf16[1,512,1024]{2,1,0:T(8,128)(2,1)} copy(bf16[1,512,1024]{2,1,0:T(8,128)(2,1)} %bitcast.4) | data formatting | bytes 2097152
  80.4 0.0 copy-done
  80.4 1.0 %copy.16 = bf16[1,512,1024]{2,1,0:T(8,128)(2,1)} copy(bf16[1,512,1024]{2,1,0:T(8,128)(2,1)S(1)} %bitcast.3) | data formatting | bytes 2097152
Async XLA Ops:
  74.9 5.4 %copy-start = (bf16[512,1024]{1,0:T(8,128)(2,1)S(1)}, bf16[512,1024]{1,0:T(8,128)(2,1)}, u32[]{:S(2)}) copy-start(bf16[512,1024]{1,0:T(8,128)(2,1)} %get-tuple-element.11) | copy-start | bytes 3145732

commit v2 on v1

--- a/solution.py
+++ b/solution.py
@@ -31,10 +31,10 @@
 
 def kernel(
     chips, dps, cap, rows,
-    place_ref, gates_ref, tok_ref, cot_ref, up_hbm, down_hbm,
-    in_ref, gate_ref, upg_ref, downg_ref,
-    tx, rx, xc, dc, actc, dhc, part, sib, xr, fin, wu, wd, ugs, ugr,
-    w_sem, ici_s, ici_r, sf_s, sf_r, xf_s, xf_r, ps_s, ps_r, xr_s, xr_r, fin_s, fin_r, ug_s, ug_r,
+    ids_ref, slots_ref, gates_ref, tok_hbm, cot_hbm, up_hbm, down_hbm,
+    in_hbm, gate_ref, upg_hbm, downg_hbm,
+    tok_ref, cot_ref, in_buf, up_buf, down_buf, tx, rx, xc, dc, actc, dhc, part, sib, xr, fin, wu, wd, ugs,
+    w_sem, out_sem, ici_s, ici_r, sf_s, sf_r, xf_s, xf_r, ps_s, ps_r, xr_s, xr_r, fin_s, fin_r, ug_s, ug_r,
 ):
     me = lax.axis_index("expert")
     k = lax.axis_index("dp")
@@ -59,8 +59,14 @@
             device_id=target, device_id_type=pl.DeviceIdType.MESH,
         )
 
+    def apart(p):
+        return p // 2 + lax.rem(p, 2) * (chips // 2)
+
+    def partner(p):
+        return xor(g, apart(p), chips)
+
     def ici(i):
-        return remote(tx.at[i], rx.at[i, c, k], ici_s.at[i], ici_r.at[i], dev(xor(g, i, chips), c, k))
+        return remote(tx.at[i], rx.at[i, c, k], ici_s.at[i], ici_r.at[i], dev(partner(i), c, k))
 
     def side(i, core, kk):
         return remote(
@@ -81,14 +87,15 @@
         )
 
     def home(i):
-        return remote(part.at[i, c, k], fin.at[i], fin_s.at[i], fin_r.at[i], dev(xor(g, i, chips), c, k))
+        return remote(part.at[i, c, k], fin.at[i], fin_s.at[i], fin_r.at[i], dev(partner(i), c, k))
 
     tile = min(256, dblk)
     tiles = dblk // tile
 
-    def up_send(j, m, kk, slot):
+    def up_send(j, m, kk, slot, col):
         return remote(
-            ugs.at[j - 1, pl.ds(m * tile, tile)], ugr.at[slot, pl.ds(m * tile, tile)],
+            ugs.at[j - 1, pl.ds(m * tile, tile)],
+            upg_hbm.at[pl.ds(m * tile, tile), pl.ds(pl.multiple_of(col * hq, hq), hq)],
             ug_s.at[kk, m], ug_r.at[slot, m], dev(g, c, kk),
         )
 
@@ -98,6 +105,10 @@
     load_down = pltpu.make_async_copy(
         down_hbm.at[0, pl.ds(pl.multiple_of(k * hq, hq), hq), :], wd, w_sem.at[1]
     )
+    load_tok = pltpu.make_async_copy(tok_hbm, tok_ref, w_sem.at[2])
+    load_cot = pltpu.make_async_copy(cot_hbm, cot_ref, w_sem.at[3])
+    load_tok.start()
+    load_cot.start()
     load_up.start()
     load_down.start()
 
@@ -108,7 +119,7 @@
 
     @pl.loop(1, chips)
     def _(i):
-        greet(dev(xor(g, i, chips), c, k))
+        greet(dev(partner(i), c, k))
 
     greet(dev(g, o, k))
     for j in range(1, dps):
@@ -120,12 +131,17 @@
     at_cap = lax.broadcasted_iota(jnp.int32, (1, rows, 128), 1) == cap
 
     def one_hot():
-        slots = lax.broadcasted_iota(jnp.int32, (chips * rows, tok_ref.shape[0]), 0)
-        return slots == place_ref[...]
+        place = ids_ref[...] * rows + slots_ref[...]
+        row = lax.broadcasted_iota(jnp.int32, (rows, place.shape[1]), 0)
+        blocks = [jnp.where(place - partner(i) * rows == row, 1.0, 0.0) for i in range(chips)]
+        return jnp.concatenate(blocks, axis=0)
 
     hot = one_hot()
-    hot16 = jnp.where(hot, 1.0, 0.0).astype(BF16)
-    gate_col = jnp.sum(jnp.where(hot, gates_ref[...].astype(F32), 0.0), axis=1, keepdims=True)
+    hot16 = hot.astype(BF16)
+    gates = gates_ref[...].astype(F32).reshape(1, -1)
+    gate_col = jnp.sum(hot * gates, axis=1, keepdims=True)
+    load_tok.wait()
+    load_cot.wait()
     gate_row = jnp.sum(jnp.where(eye, gate_col.reshape(chips, rows, 1), 0.0), axis=1, keepdims=True)
     x_pack = dot(hot16, tok_ref[...], 1, 0).reshape(chips, rows, width)
     g_pack = dot(hot16, cot_ref[...], 1, 0).reshape(chips, rows, width)
@@ -189,8 +205,10 @@
             kk = other(j)
             half_sum(i, kk).wait_recv()
             part[i, c, kk] = (part[i, c, kk].astype(F32) + sib[i, kk].astype(F32)).astype(BF16)
-            if j:
-                cross_sum(i, kk, dps - 1 - j).start()
+
+    def stage_x(i):
+        for j in range(1, dps):
+            cross_sum(i, other(j), dps - 1 - j).start()
 
     def stage_e(i):
         total = part[i, c, k].astype(F32)
@@ -217,6 +235,14 @@
         def _():
             stage_a(t)
 
+        @pl.when(t == chips - 1)
+        def _():
+            pl.loop(0, chips - 4)(stage_x)
+
+        @pl.when(t >= chips)
+        def _():
+            stage_x(t - 4)
+
         @pl.when(jnp.logical_and(t >= 1, t < chips + 1))
         def _():
             stage_b(t - 1)
@@ -229,11 +255,9 @@
         def _():
             stage_d(t - 3)
 
-        @pl.when(t >= 4)
-        def _():
-            stage_e(t - 4)
-
+    stage_x(chips - 2)
     stage_d(chips - 1)
+    stage_x(chips - 1)
 
     def up_tile(kk, m):
         at = pl.ds(pl.multiple_of(kk * dblk + m * tile, tile), tile)
@@ -243,47 +267,52 @@
         @pl.loop(0, tiles)
         def _(m):
             ugs[j - 1, pl.ds(pl.multiple_of(m * tile, tile), tile), :] = up_tile(other(j), m)
-            up_send(j, m, other(j), dps - 1 - j).start()
-
-    stage_e(chips - 2)
-    stage_e(chips - 1)
-    mine = pl.ds(pl.multiple_of(k * hq, hq), hq)
+            up_send(j, m, other(j), dps - 1 - j, k).start()
+
+    pl.loop(0, chips // 2)(stage_e)
 
     @pl.loop(0, tiles)
     def _(m):
-        upg_ref[pl.ds(pl.multiple_of(m * tile, tile), tile), mine] = up_tile(k, m)
-
+        up_buf[pl.ds(pl.multiple_of(m * tile, tile), tile), :] = up_tile(k, m)
+
+    mine = pl.ds(pl.multiple_of(k * hq, hq), hq)
+    put_up = pltpu.make_async_copy(up_buf, upg_hbm.at[:, mine], out_sem.at[0])
+    put_up.start()
     dtile = min(256, hq)
 
     @pl.loop(0, hq // dtile)
     def _(m):
         at = pl.ds(pl.multiple_of(m * dtile, dtile), dtile)
-        downg_ref[at, :] = dot(actc[:, at], dc[...], 0, 0).astype(BF16)
+        down_buf[at, :] = dot(actc[:, at], dc[...], 0, 0).astype(BF16)
+
+    put_down = pltpu.make_async_copy(down_buf, downg_hbm, out_sem.at[1])
+    put_down.start()
+    pl.loop(chips // 2, chips)(stage_e)
 
     @pl.loop(1, chips)
     def _(i):
         home(i).wait_recv()
 
     hot = one_hot()
-    hot16 = jnp.where(hot, 1.0, 0.0).astype(BF16)
+    hot16 = hot.astype(BF16)
     back = fin[...].astype(F32)
     left = back[:, :rows].reshape(chips * rows, half).astype(BF16)
     right = back[:, rows:].reshape(chips * rows, half).astype(BF16)
-    in_ref[:, :half] = dot(hot16, left, 0, 0).astype(BF16)
-    in_ref[:, half:] = dot(hot16, right, 0, 0).astype(BF16)
+    in_buf[:, :half] = dot(hot16, left, 0, 0).astype(BF16)
+    in_buf[:, half:] = dot(hot16, right, 0, 0).astype(BF16)
     col = jnp.sum(
         jnp.where(eye, back[:, cap : cap + 1, :128], 0.0), axis=2, keepdims=True
     ).reshape(chips * rows, 1)
-    gate_ref[...] = jnp.sum(jnp.where(hot, col, 0.0), axis=0, keepdims=True).astype(BF16)
+    gate_ref[...] = jnp.sum(hot * col, axis=0).astype(BF16)
+    put_in = pltpu.make_async_copy(in_buf, in_hbm, out_sem.at[2])
+    put_in.start()
 
     for j in range(1, dps):
         kk = other(j)
 
         @pl.loop(0, tiles)
         def _(m):
-            up_send(j, m, kk, j - 1).wait_recv()
-
-        upg_ref[:, pl.ds(pl.multiple_of(kk * hq, hq), hq)] = ugr[j - 1]
+            up_send(j, m, kk, j - 1, kk).wait_recv()
 
     @pl.loop(0, chips)
     def _(i):
@@ -302,7 +331,22 @@
     for j in range(1, dps):
         @pl.loop(0, tiles)
         def _(m):
-            up_send(j, m, other(j), dps - 1 - j).wait_send()
+            up_send(j, m, other(j), dps - 1 - j, k).wait_send()
+
+    put_up.wait()
+    put_down.wait()
+    put_in.wait()
+
+
+def hand_on(*refs):
+    count = len(refs) // 2
+    copies = [
+        pltpu.make_async_copy(refs[n], refs[count + n], refs[-1].at[n]) for n in range(count)
+    ]
+    for copy in copies:
+        copy.start()
+    for copy in copies:
+        copy.wait()
 
 
 def on_device(tokens_in, out_grad, gates, expert_ids, slot_ids, w_up, w_down):
@@ -314,24 +358,27 @@
     rows = (cap + 1 + 7) // 8 * 8
     hq = hidden // dps
     dblk = width // dps
-    g = lax.axis_index("expert") // 2
-    place = (jnp.bitwise_xor(expert_ids, g) * rows + slot_ids).reshape(1, tokens)
     slots = 2 * dps * chips * rows
     tiles = dblk // min(256, dblk)
     vmem = pl.BlockSpec(memory_space=pltpu.VMEM)
     hbm = pl.BlockSpec(memory_space=pl.ANY)
     dma = pltpu.SemaphoreType.DMA
-    in_grad, gate_grad, up_grad, down_grad = pl.pallas_call(
+    raw = pl.pallas_call(
         functools.partial(kernel, chips, dps, cap, rows),
         out_shape=(
             jax.ShapeDtypeStruct((tokens, width), BF16),
-            jax.ShapeDtypeStruct((1, tokens), BF16),
+            jax.ShapeDtypeStruct((tokens,), BF16),
             jax.ShapeDtypeStruct((dblk, hidden), BF16),
             jax.ShapeDtypeStruct((hq, width), BF16),
         ),
-        in_specs=[vmem] * 4 + [hbm] * 2,
-        out_specs=(vmem,) * 4,
+        in_specs=[vmem] * 3 + [hbm] * 4,
+        out_specs=(hbm, vmem, hbm, hbm),
         scratch_shapes=[
+            pltpu.VMEM((tokens, width), BF16),
+            pltpu.VMEM((tokens, width), BF16),
+            pltpu.VMEM((tokens, width), BF16),
+            pltpu.VMEM((dblk, hq), BF16),
+            pltpu.VMEM((hq, width), BF16),
             pltpu.VMEM((chips, 2 * rows, width), BF16),
             pltpu.VMEM((chips, 2, dps, 2 * rows, width), BF16),
             pltpu.VMEM((slots, width), BF16),
@@ -345,8 +392,8 @@
             pltpu.VMEM((width, hq), BF16),
             pltpu.VMEM((hq, width), BF16),
             pltpu.VMEM((dps - 1, dblk, hq), BF16),
-            pltpu.VMEM((dps - 1, dblk, hq), BF16),
-            dma((2,)),
+            dma((4,)),
+            dma((3,)),
             dma((chips,)),
             dma((chips,)),
             dma((chips, dps)),
@@ -365,8 +412,18 @@
         compiler_params=pltpu.CompilerParams(
             collective_id=0, has_side_effects=True, vmem_limit_bytes=61 * 1024 * 1024
         ),
-    )(place, gates.reshape(1, tokens), tokens_in, out_grad, w_up, w_down)
-    return (in_grad, gate_grad.reshape(tokens), up_grad[None], down_grad[None])
+    )(
+        expert_ids.reshape(1, tokens), slot_ids.reshape(1, tokens), gates,
+        tokens_in, out_grad, w_up, w_down,
+    )
+    in_grad, gate_grad, up_grad, down_grad = pl.pallas_call(
+        hand_on,
+        out_shape=[jax.ShapeDtypeStruct(r.shape, r.dtype) for r in raw],
+        in_specs=[hbm] * 4,
+        out_specs=[hbm] * 4,
+        scratch_shapes=[dma((4,))],
+    )(*raw)
+    return (in_grad, gate_grad, up_grad[None], down_grad[None])
 
 
 def solution(mesh):

time: 81.6 us -> 155 us (1.90)
  Pallas kernels: 71.8 us -> 154 us
  local copies, waits for them, and re-layouts: 6.32 us -> 0 us
  other arithmetic: 2.55 us -> 0 us
    pallas_call x0 -> x1, Pallas kernels: none -> 80.6 us  [on_device(): pl.pallas_call(hand_on, out_shape=[jax.ShapeDtypeStruct(r.shape, r.dtype)...]
    unnamed x5 -> x0, local copies, waits for them, and re-layouts: 5.1 us -> none
where the time goes in v2:
time: 155 us; the launch traced here: 154 us
  Pallas kernels  154 us (99%)
    pallas_call x1, Pallas kernels, on_device(): pl.pallas_call(hand_on, out_shape=[jax.ShapeDtypeStruct(r.shape, r.dtype)...  80.6 us
    pallas_call x1, Pallas kernels, on_device(): pl.pallas_call(functools.partial(kernel, chips, dps, cap, rows), out_shap...  73.2 us

profile of v2, /device:TPU:0, one launch (start us, length us, event | category | flops | bytes accessed | tf_op | source)
XLA Modules:
  0.0 154.4 jit_solution(1854163944257348467)
XLA Ops:
  0.6 73.2 %shard_map.102 = (bf16[256,1024]{1,0:T(8,128)(2,1)}, bf16[256]{0:T(256)(128)(2,1)}, bf16[512,1024]{1,0:T(8,128)(2,1)}, bf16[512,1024]{1,0:T(8,128)(2,1)}) custom-call(s32[1,256]{1,0:T(1,128)} %bitcast.4, s32[1,256]{1,0:T(1,128)} %bitcast.5, bf16[256]{0:T(256)(128)(2,1)} %gates_ref.1, bf16[256,1024]{1,0:T(8,128)(2,1)} %tok_hbm.1, bf16[256,1024]{1,0:T(8,128)(2,1)} %cot_hbm.1, ...), custom_call_target="tpu_custom_call" | custom-call | tf_op jit(solution)/shard_map/pallas_call | solution.py:366
  73.9 80.6 %shard_map.103 = (bf16[256,1024]{1,0:T(8,128)(2,1)}, bf16[256]{0:T(256)(128)(2,1)}, bf16[512,1024]{1,0:T(8,128)(2,1)}, bf16[512,1024]{1,0:T(8,128)(2,1)}) custom-call(bf16[256,1024]{1,0:T(8,128)(2,1)} %get-tuple-element.12.refs_0_, bf16[256]{0:T(256)(128)(2,1)} %get-tuple-element.13.refs_1_, bf16[512,1024]{1,0:T(8,128)(2,1)} %get-tuple-element.14.refs_2_, ...), custom_call_target="tpu_custom_call" | custom-call | tf_op jit(solution)/shard_map/pallas_call | solution.py:419

commit v3 on v2

v3 whole, which is shorter than its diff:
```python
import functools

import jax
import jax.numpy as jnp
from jax import lax
from jax.experimental import pallas as pl
from jax.experimental.pallas import tpu as pltpu
from jax.sharding import PartitionSpec as P

F32 = jnp.float32
BF16 = jnp.bfloat16


def xor(a, b, count):
    total, bit = 0, 1
    while bit < count:
        total = total + lax.rem(a // bit + b // bit, 2) * bit
        bit *= 2
    return total


def gelu_parts(hidden):
    cdf = 0.5 * (1.0 + lax.erf(hidden * 0.7071067811865476))
    pdf = jnp.exp(-0.5 * hidden * hidden) * 0.3989422804014327
    return (hidden * cdf, cdf + hidden * pdf)


def dot(a, b, da, db):
    return lax.dot_general(a, b, (((da,), (db,)), ((), ())), preferred_element_type=F32)


def kernel(
    chips, dps, cap, rows,
    ids_ref, slots_ref, gates_ref, tok_hbm, cot_hbm, up_hbm, down_hbm,
    in_hbm, gate_ref, upg_hbm, downg_hbm,
    tok_ref, cot_ref, in_buf, up_buf, down_buf, tx, rx, xc, dc, actc, dhc, act_tmp, dh_tmp,
    part, sib, fin, wu, wd, ugs,
    w_sem, out_sem, ici_s, ici_r, sf_s, sf_r, xf_s, xf_r, ps_s, ps_r, fin_s, fin_r, ug_s, ug_r,
):
    me = lax.axis_index("expert")
    k = lax.axis_index("dp")
    g = me // 2
    c = lax.rem(me, 2)
    o = 1 - c
    tokens, width = tok_ref.shape
    half = width // 2
    hidden_dev = wu.shape[1]
    hq = hidden_dev // dps
    dblk = width // dps
    full = rows - 8
    pairs = chips // 2
    own_per = 4 * rows
    other_per = own_per * (dps - 1)
    mine = pl.ds(pl.multiple_of(k * hq, hq), hq)

    def dev(chip, core, dp):
        return {"expert": chip * 2 + core, "dp": dp}

    def other(j):
        return lax.rem(k + j, dps)

    def remote(src, dst, s, r, target):
        return pltpu.make_async_remote_copy(
            src_ref=src, dst_ref=dst, send_sem=s, recv_sem=r,
            device_id=target, device_id_type=pl.DeviceIdType.MESH,
        )

    def partner(p):
        return xor(g, p // 2 + lax.rem(p, 2) * (chips // 2), chips)

    def ici(i):
        return remote(tx.at[i], rx.at[k, i, c], ici_s.at[i], ici_r.at[i], dev(partner(i), c, k))

    def side(i, core, kk):
        return remote(
            rx.at[kk, i, core], rx.at[kk, i, core], sf_s.at[i, kk], sf_r.at[i, kk], dev(g, o, k)
        )

    def cross(i, kk, slot):
        return remote(
            rx.at[slot, i, c], rx.at[slot, i, c], xf_s.at[i, kk], xf_r.at[i, slot], dev(g, c, kk)
        )

    def half_sum(i):
        return remote(part.at[i, o], sib.at[i], ps_s.at[i], ps_r.at[i], dev(g, o, k))

    def home(i):
        return remote(part.at[i, c], fin.at[i], fin_s.at[i], fin_r.at[i], dev(partner(i), c, k))

    tile = min(256, dblk)
    tiles = dblk // tile

    def up_send(j, m, kk, slot, col):
        return remote(
            ugs.at[j - 1, pl.ds(m * tile, tile)],
            upg_hbm.at[pl.ds(m * tile, tile), pl.ds(pl.multiple_of(col * hq, hq), hq)],
            ug_s.at[kk, m], ug_r.at[slot, m], dev(g, c, kk),
        )

    load_tok = pltpu.make_async_copy(tok_hbm, tok_ref, w_sem.at[2])
    load_cot = pltpu.make_async_copy(cot_hbm, cot_ref, w_sem.at[3])
    load_up = pltpu.make_async_copy(up_hbm.at[0], wu, w_sem.at[0])
    load_down = pltpu.make_async_copy(down_hbm.at[0], wd, w_sem.at[1])
    load_tok.start()
    load_cot.start()
    load_up.start()
    load_down.start()

    barrier = pltpu.get_barrier_semaphore()

    def greet(target):
        pl.semaphore_signal(barrier, inc=1, device_id=target, device_id_type=pl.DeviceIdType.MESH)

    @pl.loop(1, chips)
    def _(i):
        greet(dev(partner(i), c, k))

    greet(dev(g, o, k))
    for j in range(1, dps):
        greet(dev(g, c, other(j)))

    eye = lax.broadcasted_iota(jnp.int32, (1, rows, 128), 1) == lax.broadcasted_iota(
        jnp.int32, (1, rows, 128), 2
    )
    at_cap = lax.broadcasted_iota(jnp.int32, (1, rows, 128), 1) == cap
    upper = lax.broadcasted_iota(jnp.int32, (1, 8, 1), 1) < 4

    def one_hot():
        place = ids_ref[...] * rows + slots_ref[...]
        row = lax.broadcasted_iota(jnp.int32, (rows, place.shape[1]), 0)
        blocks = [jnp.where(place - partner(i) * rows == row, 1.0, 0.0) for i in range(chips)]
        return jnp.concatenate(blocks, axis=0)

    def rolled(tiles8, shift):
        count = tiles8.shape[0]
        flat = pltpu.roll(tiles8.reshape(count * 8, width), shift, 0)
        return flat.reshape(count, 8, width)

    hot = one_hot()
    hot16 = hot.astype(BF16)
    gates = gates_ref[...].astype(F32).reshape(1, -1)
    gate_col = jnp.sum(hot * gates, axis=1, keepdims=True)
    load_tok.wait()
    load_cot.wait()
    x_pack = dot(hot16, tok_ref[...], 1, 0).reshape(chips, rows, width)
    d_pack = (dot(hot16, cot_ref[...], 1, 0) * gate_col).reshape(chips, rows, width)
    mixed = jnp.where(upper, x_pack[:, full:], rolled(d_pack[:, full:], 4))
    both = jnp.concatenate([x_pack[:, :full], mixed, d_pack[:, :full]], axis=1).astype(BF16)
    tx[...] = both
    rx[k, 0, c] = both[0]

    pl.semaphore_wait(barrier, chips - 1 + 1 + dps - 1)

    @pl.loop(1, chips)
    def _(i):
        ici(i).start()

    def stage_a(i):
        @pl.when(i > 0)
        def _():
            ici(i).wait_recv()

        for j in range(1, dps):
            cross(i, other(j), k).start()
        side(i, c, k).start()

    def stage_b(i):
        for j in range(1, dps):
            cross(i, other(j), other(j)).wait_recv()
            side(i, c, other(j)).start()

    def unpack(blk):
        blk = blk.astype(F32)
        count = blk.shape[0]
        mid = blk[:, full : full + 8]
        x_last = jnp.where(upper, mid, 0.0)
        d_last = jnp.where(upper, rolled(mid, count * 8 - 4), 0.0)
        x = jnp.concatenate([blk[:, :full], x_last], axis=1)
        d = jnp.concatenate([blk[:, full + 8 :], d_last], axis=1)
        return (
            x.reshape(count * rows, width).astype(BF16),
            d.reshape(count * rows, width).astype(BF16),
        )

    def stage_c(t):
        side(2 * t, o, k).wait_recv()
        side(2 * t + 1, o, k).wait_recv()
        x, d = unpack(rx[k, pl.ds(2 * t, 2)].reshape(4, 2 * full + 8, width))
        at = pl.ds(pl.multiple_of(t * own_per, own_per), own_per)
        xc[at, :] = x
        dc[at, :] = d
        value, slope = gelu_parts(dot(x, wu[...], 1, 0))
        d_act = dot(d, wd[...], 1, 1)
        act = value.astype(BF16)
        dh = (d_act * slope).astype(BF16)
        act_tmp[...] = act
        dh_tmp[...] = dh
        actc[at, :] = act_tmp[:, mine]
        dhc[at, :] = dh_tmp[:, mine]
        gp = jnp.sum(act.astype(F32) * d_act, axis=1, keepdims=True).reshape(4, rows, 1)
        gp_row = jnp.sum(jnp.where(eye, gp, 0.0), axis=1, keepdims=True)
        d_in = dot(dh, wu[...], 1, 1).reshape(4, rows, width)
        lead = jnp.where(at_cap, gp_row, d_in[:, :, :128])
        left = jnp.concatenate([lead, d_in[:, :, 128:half]], axis=2)
        whole = jnp.concatenate([left, d_in[:, :, half:]], axis=1).astype(BF16)
        part[pl.ds(2 * t, 2)] = whole.reshape(2, 2, 2 * rows, half)
        half_sum(2 * t).start()
        half_sum(2 * t + 1).start()

    def stage_o(t):
        for j in range(1, dps):
            kk = other(j)
            side(2 * t, o, kk).wait_recv()
            side(2 * t + 1, o, kk).wait_recv()
            x, d = unpack(rx[kk, pl.ds(2 * t, 2)].reshape(4, 2 * full + 8, width))
            at = pl.ds(
                pl.multiple_of(pairs * own_per + t * other_per + (j - 1) * own_per, own_per), own_per
            )
            xc[at, :] = x
            dc[at, :] = d
            value, slope = gelu_parts(dot(x, wu[:, mine], 1, 0))
            d_act = dot(d, wd[mine, :], 1, 1)
            actc[at, :] = value.astype(BF16)
            dhc[at, :] = (d_act * slope).astype(BF16)

    def stage_e(i):
        half_sum(i).wait_recv()
        total = (part[i, c].astype(F32) + sib[i].astype(F32)).astype(BF16)

        @pl.when(i > 0)
        def _():
            part[i, c] = total
            home(i).start()

        @pl.when(i == 0)
        def _():
            fin[0] = total

    stage_a(0)
    load_up.wait()
    load_down.wait()

    @pl.loop(0, pairs)
    def _(t):
        @pl.when(t > 0)
        def _():
            stage_a(2 * t)

        stage_a(2 * t + 1)

        @pl.when(t >= 1)
        def _():
            stage_c(t - 1)
            stage_b(2 * t - 2)
            stage_b(2 * t - 1)

        @pl.when(t >= 2)
        def _():
            stage_o(t - 2)

    pl.loop(0, chips - 2)(stage_e)
    stage_c(pairs - 1)
    stage_b(chips - 2)
    stage_b(chips - 1)
    stage_o(pairs - 2)
    stage_e(chips - 2)
    stage_e(chips - 1)
    stage_o(pairs - 1)

    def up_tile(kk, m):
        at = pl.ds(pl.multiple_of(kk * dblk + m * tile, tile), tile)
        return dot(xc[:, at], dhc[...], 0, 0).astype(BF16)

    for j in range(1, dps):
        @pl.loop(0, tiles)
        def _(m):
            ugs[j - 1, pl.ds(pl.multiple_of(m * tile, tile), tile), :] = up_tile(other(j), m)
            up_send(j, m, other(j), dps - 1 - j, k).start()

    @pl.loop(0, tiles)
    def _(m):
        up_buf[pl.ds(pl.multiple_of(m * tile, tile), tile), :] = up_tile(k, m)

    put_up = pltpu.make_async_copy(up_buf, upg_hbm.at[:, mine], out_sem.at[0])
    put_up.start()
    dtile = min(256, hq)

    @pl.loop(0, hq // dtile)
    def _(m):
        at = pl.ds(pl.multiple_of(m * dtile, dtile), dtile)
        down_buf[at, :] = dot(actc[:, at], dc[...], 0, 0).astype(BF16)

    put_down = pltpu.make_async_copy(down_buf, downg_hbm, out_sem.at[1])
    put_down.start()

    @pl.loop(1, chips)
    def _(i):
        home(i).wait_recv()

    hot = one_hot()
    hot16 = hot.astype(BF16)
    back = fin[...].astype(F32)
    left = back[:, :rows].reshape(chips * rows, half).astype(BF16)
    right = back[:, rows:].reshape(chips * rows, half).astype(BF16)
    in_buf[:, :half] = dot(hot16, left, 0, 0).astype(BF16)
    in_buf[:, half:] = dot(hot16, right, 0, 0).astype(BF16)
    put_in = pltpu.make_async_copy(in_buf, in_hbm, out_sem.at[2])
    put_in.start()
    col = jnp.sum(
        jnp.where(eye, back[:, cap : cap + 1, :128], 0.0), axis=2, keepdims=True
    ).reshape(chips * rows, 1)
    scaled = jnp.sum(hot * col, axis=0, keepdims=True)
    gate_ref[...] = (scaled / gates_ref[...].astype(F32).reshape(1, -1)).astype(BF16).reshape(tokens)

    @pl.loop(0, chips)
    def _(i):
        @pl.when(i > 0)
        def _():
            ici(i).wait_send()
            home(i).wait_send()

        half_sum(i).wait_send()
        for kk in range(dps):
            side(i, c, kk).wait_send()
        for j in range(1, dps):
            cross(i, other(j), k).wait_send()

    for j in range(1, dps):
        kk = other(j)

        @pl.loop(0, tiles)
        def _(m):
            up_send(j, m, kk, j - 1, kk).wait_recv()
            up_send(j, m, kk, dps - 1 - j, k).wait_send()

    put_up.wait()
    put_down.wait()
    put_in.wait()


def hand_on(a, b, c, d, a_out, b_out, c_out, d_out, a_buf, b_buf, c_buf, d_buf, sems):
    buffers = (a_buf, b_buf, c_buf, d_buf)
    ins = [
        pltpu.make_async_copy(ref, buf, sems.at[0, n])
        for n, (ref, buf) in enumerate(zip((a, b, c, d), buffers))
    ]
    outs = [
        pltpu.make_async_copy(buf, ref, sems.at[1, n])
        for n, (ref, buf) in enumerate(zip((a_out, b_out, c_out, d_out), buffers))
    ]
    for copy in ins:
        copy.start()
    for first, then in zip(ins, outs):
        first.wait()
        then.start()
    for copy in outs:
        copy.wait()


def on_device(tokens_in, out_grad, gates, expert_ids, slot_ids, w_up, w_down):
    chips = lax.axis_size("expert") // 2
    dps = lax.axis_size("dp")
    tokens, width = tokens_in.shape
    hidden = w_up.shape[2]
    cap = 9 * tokens // (8 * chips)
    assert 1 <= cap % 8 <= 4
    rows = cap // 8 * 8 + 8
    hq = hidden // dps
    dblk = width // dps
    slots = 2 * dps * chips * rows
    tiles = dblk // min(256, dblk)
    vmem = pl.BlockSpec(memory_space=pltpu.VMEM)
    hbm = pl.BlockSpec(memory_space=pl.ANY)
    dma = pltpu.SemaphoreType.DMA
    raw = pl.pallas_call(
        functools.partial(kernel, chips, dps, cap, rows),
        out_shape=(
            jax.ShapeDtypeStruct((tokens, width), BF16),
            jax.ShapeDtypeStruct((tokens,), BF16),
            jax.ShapeDtypeStruct((dblk, hidden), BF16),
            jax.ShapeDtypeStruct((hq, width), BF16),
        ),
        in_specs=[vmem] * 3 + [hbm] * 4,
        out_specs=(hbm, vmem, hbm, hbm),
        scratch_shapes=[
            pltpu.VMEM((tokens, width), BF16),
            pltpu.VMEM((tokens, width), BF16),
            pltpu.VMEM((tokens, width), BF16),
            pltpu.VMEM((dblk, hq), BF16),
            pltpu.VMEM((hq, width), BF16),
            pltpu.VMEM((chips, 2 * rows - 8, width), BF16),
            pltpu.VMEM((dps, chips, 2, 2 * rows - 8, width), BF16),
            pltpu.VMEM((slots, width), BF16),
            pltpu.VMEM((slots, width), BF16),
            pltpu.VMEM((slots, hq), BF16),
            pltpu.VMEM((slots, hq), BF16),
            pltpu.VMEM((4 * rows, hidden), BF16),
            pltpu.VMEM((4 * rows, hidden), BF16),
            pltpu.VMEM((chips, 2, 2 * rows, width // 2), BF16),
            pltpu.VMEM((chips, 2 * rows, width // 2), BF16),
            pltpu.VMEM((chips, 2 * rows, width // 2), BF16),
            pltpu.VMEM((width, hidden), BF16),
            pltpu.VMEM((hidden, width), BF16),
            pltpu.VMEM((dps - 1, dblk, hq), BF16),
            dma((4,)),
            dma((3,)),
            dma((chips,)),
            dma((chips,)),
            dma((chips, dps)),
            dma((chips, dps)),
            dma((chips, dps)),
            dma((chips, dps)),
            dma((chips,)),
            dma((chips,)),
            dma((chips,)),
            dma((chips,)),
            dma((dps, tiles)),
            dma((dps, tiles)),
        ],
        compiler_params=pltpu.CompilerParams(
            collective_id=0, has_side_effects=True, vmem_limit_bytes=61 * 1024 * 1024
        ),
    )(
        expert_ids.reshape(1, tokens), slot_ids.reshape(1, tokens), gates,
        tokens_in, out_grad, w_up, w_down,
    )
    in_grad, gate_grad, up_grad, down_grad = pl.pallas_call(
        hand_on,
        out_shape=[jax.ShapeDtypeStruct(r.shape, r.dtype) for r in raw],
        in_specs=[hbm] * 4,
        out_specs=[hbm] * 4,
        scratch_shapes=[pltpu.VMEM(r.shape, r.dtype) for r in raw] + [dma((2, 4))],
    )(*raw)
    return (in_grad, gate_grad, up_grad[None], down_grad[None])


def solution(mesh):
    return jax.shard_map(
        on_device,
        mesh=mesh,
        in_specs=(
            P(("expert", "dp"), None),
            P(("expert", "dp"), None),
            P(("expert", "dp")),
            P(("expert", "dp")),
            P(("expert", "dp")),
            P("expert", None, None),
            P("expert", None, None),
        ),
        out_specs=(
            P(("expert", "dp"), None),
            P(("expert", "dp")),
            P("expert", "dp", None),
            P("expert", "dp", None),
        ),
        check_vma=False,
    )
```

time: 155 us -> 62.5 us (0.40)
  Pallas kernels: 154 us -> 61.7 us
    pallas_call x1, Pallas kernels: 80.6 us -> 2.78 us  [on_device(): pl.pallas_call(hand_on, out_shape=[jax.ShapeDtypeStruct(r.shape, r.dtype)...]
    pallas_call x1, Pallas kernels: 73.2 us -> 58.9 us  [on_device(): pl.pallas_call(functools.partial(kernel, chips, dps, cap, rows), out_shap...]
where the time goes in v3:
time: 62.5 us; the launch traced here: 62.3 us
  Pallas kernels  61.7 us (99%)
  between operations  0.64 us (1%)
    pallas_call x1, Pallas kernels, on_device(): pl.pallas_call(functools.partial(kernel, chips, dps, cap, rows), out_shap...  58.9 us
    pallas_call x1, Pallas kernels, on_device(): pl.pallas_call(hand_on, out_shape=[jax.ShapeDtypeStruct(r.shape, r.dtype)...  2.78 us

profile of v3, /device:TPU:0, one launch (start us, length us, event | category | flops | bytes accessed | tf_op | source)
XLA Modules:
  0.0 62.3 jit_solution(6131580852653156680)
XLA Ops:
  0.6 58.9 %shard_map.102 = (bf16[256,1024]{1,0:T(8,128)(2,1)}, bf16[256]{0:T(256)(128)(2,1)}, bf16[512,1024]{1,0:T(8,128)(2,1)}, bf16[512,1024]{1,0:T(8,128)(2,1)}) custom-call(s32[1,256]{1,0:T(1,128)} %bitcast.4, s32[1,256]{1,0:T(1,128)} %bitcast.5, bf16[256]{0:T(256)(128)(2,1)} %gates_ref.1, bf16[256,1024]{1,0:T(8,128)(2,1)} %tok_hbm.1, bf16[256,1024]{1,0:T(8,128)(2,1)} %cot_hbm.1, ...), custom_call_target="tpu_custom_call" | custom-call | tf_op jit(solution)/shard_map/pallas_call | solution.py:375
  59.5 2.8 %shard_map.103 = (bf16[256,1024]{1,0:T(8,128)(2,1)}, bf16[256]{0:T(256)(128)(2,1)}, bf16[512,1024]{1,0:T(8,128)(2,1)}, bf16[512,1024]{1,0:T(8,128)(2,1)}) custom-call(bf16[256,1024]{1,0:T(8,128)(2,1)} %get-tuple-element.12.a, bf16[256]{0:T(256)(128)(2,1)} %get-tuple-element.13.b, bf16[512,1024]{1,0:T(8,128)(2,1)} %get-tuple-element.14.c, ...), custom_call_target="tpu_custom_call" | custom-call | tf_op jit(solution)/shard_map/pallas_call | solution.py:427

commit v4 on v3

--- a/solution.py
+++ b/solution.py
@@ -32,10 +32,10 @@
 def kernel(
     chips, dps, cap, rows,
     ids_ref, slots_ref, gates_ref, tok_hbm, cot_hbm, up_hbm, down_hbm,
-    in_hbm, gate_ref, upg_hbm, downg_hbm,
-    tok_ref, cot_ref, in_buf, up_buf, down_buf, tx, rx, xc, dc, actc, dhc, act_tmp, dh_tmp,
-    part, sib, fin, wu, wd, ugs,
-    w_sem, out_sem, ici_s, ici_r, sf_s, sf_r, xf_s, xf_r, ps_s, ps_r, fin_s, fin_r, ug_s, ug_r,
+    fin, upg_hbm, downg_hbm,
+    tok_ref, cot_ref, up_buf, down_buf, tx, rx, xc, dc, actc, dhc, act_tmp,
+    part, sib, wu, wd,
+    w_sem, out_sem, ici_s, ici_r, sf_s, sf_r, xf_s, xf_r, ps_s, ps_r, fin_s, fin_r,
 ):
     me = lax.axis_index("expert")
     k = lax.axis_index("dp")
@@ -66,7 +66,7 @@
         )
 
     def partner(p):
-        return xor(g, p // 2 + lax.rem(p, 2) * (chips // 2), chips)
+        return xor(g, p, chips)
 
     def ici(i):
         return remote(tx.at[i], rx.at[k, i, c], ici_s.at[i], ici_r.at[i], dev(partner(i), c, k))
@@ -86,16 +86,6 @@
 
     def home(i):
         return remote(part.at[i, c], fin.at[i], fin_s.at[i], fin_r.at[i], dev(partner(i), c, k))
-
-    tile = min(256, dblk)
-    tiles = dblk // tile
-
-    def up_send(j, m, kk, slot, col):
-        return remote(
-            ugs.at[j - 1, pl.ds(m * tile, tile)],
-            upg_hbm.at[pl.ds(m * tile, tile), pl.ds(pl.multiple_of(col * hq, hq), hq)],
-            ug_s.at[kk, m], ug_r.at[slot, m], dev(g, c, kk),
-        )
 
     load_tok = pltpu.make_async_copy(tok_hbm, tok_ref, w_sem.at[2])
     load_cot = pltpu.make_async_copy(cot_hbm, cot_ref, w_sem.at[3])
@@ -125,18 +115,12 @@
     at_cap = lax.broadcasted_iota(jnp.int32, (1, rows, 128), 1) == cap
     upper = lax.broadcasted_iota(jnp.int32, (1, 8, 1), 1) < 4
 
-    def one_hot():
-        place = ids_ref[...] * rows + slots_ref[...]
-        row = lax.broadcasted_iota(jnp.int32, (rows, place.shape[1]), 0)
-        blocks = [jnp.where(place - partner(i) * rows == row, 1.0, 0.0) for i in range(chips)]
-        return jnp.concatenate(blocks, axis=0)
-
     def rolled(tiles8, shift):
         count = tiles8.shape[0]
         flat = pltpu.roll(tiles8.reshape(count * 8, width), shift, 0)
         return flat.reshape(count, 8, width)
 
-    hot = one_hot()
+    hot = one_hot(ids_ref, slots_ref, g, chips, rows)
     hot16 = hot.astype(BF16)
     gates = gates_ref[...].astype(F32).reshape(1, -1)
     gate_col = jnp.sum(hot * gates, axis=1, keepdims=True)
@@ -151,9 +135,12 @@
 
     pl.semaphore_wait(barrier, chips - 1 + 1 + dps - 1)
 
-    @pl.loop(1, chips)
+    ici(chips // 2).start()
+
+    @pl.loop(1, chips // 2)
     def _(i):
         ici(i).start()
+        ici(chips // 2 + i).start()
 
     def stage_a(i):
         @pl.when(i > 0)
@@ -194,9 +181,8 @@
         act = value.astype(BF16)
         dh = (d_act * slope).astype(BF16)
         act_tmp[...] = act
-        dh_tmp[...] = dh
         actc[at, :] = act_tmp[:, mine]
-        dhc[at, :] = dh_tmp[:, mine]
+        dhc[at, :] = dh
         gp = jnp.sum(act.astype(F32) * d_act, axis=1, keepdims=True).reshape(4, rows, 1)
         gp_row = jnp.sum(jnp.where(eye, gp, 0.0), axis=1, keepdims=True)
         d_in = dot(dh, wu[...], 1, 1).reshape(4, rows, width)
@@ -218,9 +204,10 @@
             )
             xc[at, :] = x
             dc[at, :] = d
-            value, slope = gelu_parts(dot(x, wu[:, mine], 1, 0))
-            d_act = dot(d, wd[mine, :], 1, 1)
-            actc[at, :] = value.astype(BF16)
+            value, slope = gelu_parts(dot(x, wu[...], 1, 0))
+            d_act = dot(d, wd[...], 1, 1)
+            act_tmp[...] = value.astype(BF16)
+            actc[at, :] = act_tmp[:, mine]
             dhc[at, :] = (d_act * slope).astype(BF16)
 
     def stage_e(i):
@@ -234,8 +221,10 @@
 
         @pl.when(i == 0)
         def _():
-            fin[0] = total
-
+            part[i, c] = total
+            put_own.start()
+
+    put_own = pltpu.make_async_copy(part.at[0, c], fin.at[0], out_sem.at[2])
     stage_a(0)
     load_up.wait()
     load_down.wait()
@@ -245,18 +234,18 @@
         @pl.when(t > 0)
         def _():
             stage_a(2 * t)
-
-        stage_a(2 * t + 1)
-
-        @pl.when(t >= 1)
-        def _():
             stage_c(t - 1)
+
+        @pl.when(t >= 2)
+        def _():
+            stage_o(t - 2)
+
+        @pl.when(t > 0)
+        def _():
             stage_b(2 * t - 2)
             stage_b(2 * t - 1)
 
-        @pl.when(t >= 2)
-        def _():
-            stage_o(t - 2)
+        stage_a(2 * t + 1)
 
     pl.loop(0, chips - 2)(stage_e)
     stage_c(pairs - 1)
@@ -267,21 +256,15 @@
     stage_e(chips - 1)
     stage_o(pairs - 1)
 
-    def up_tile(kk, m):
-        at = pl.ds(pl.multiple_of(kk * dblk + m * tile, tile), tile)
-        return dot(xc[:, at], dhc[...], 0, 0).astype(BF16)
-
-    for j in range(1, dps):
-        @pl.loop(0, tiles)
-        def _(m):
-            ugs[j - 1, pl.ds(pl.multiple_of(m * tile, tile), tile), :] = up_tile(other(j), m)
-            up_send(j, m, other(j), dps - 1 - j, k).start()
-
-    @pl.loop(0, tiles)
+    tile = min(256, dblk)
+
+    @pl.loop(0, dblk // tile)
     def _(m):
-        up_buf[pl.ds(pl.multiple_of(m * tile, tile), tile), :] = up_tile(k, m)
-
-    put_up = pltpu.make_async_copy(up_buf, upg_hbm.at[:, mine], out_sem.at[0])
+        at = pl.ds(pl.multiple_of(k * dblk + m * tile, tile), tile)
+        to = pl.ds(pl.multiple_of(m * tile, tile), tile)
+        up_buf[to, :] = dot(xc[:, at], dhc[...], 0, 0).astype(BF16)
+
+    put_up = pltpu.make_async_copy(up_buf, upg_hbm, out_sem.at[0])
     put_up.start()
     dtile = min(256, hq)
 
@@ -296,21 +279,6 @@
     @pl.loop(1, chips)
     def _(i):
         home(i).wait_recv()
-
-    hot = one_hot()
-    hot16 = hot.astype(BF16)
-    back = fin[...].astype(F32)
-    left = back[:, :rows].reshape(chips * rows, half).astype(BF16)
-    right = back[:, rows:].reshape(chips * rows, half).astype(BF16)
-    in_buf[:, :half] = dot(hot16, left, 0, 0).astype(BF16)
-    in_buf[:, half:] = dot(hot16, right, 0, 0).astype(BF16)
-    put_in = pltpu.make_async_copy(in_buf, in_hbm, out_sem.at[2])
-    put_in.start()
-    col = jnp.sum(
-        jnp.where(eye, back[:, cap : cap + 1, :128], 0.0), axis=2, keepdims=True
-    ).reshape(chips * rows, 1)
-    scaled = jnp.sum(hot * col, axis=0, keepdims=True)
-    gate_ref[...] = (scaled / gates_ref[...].astype(F32).reshape(1, -1)).astype(BF16).reshape(tokens)
 
     @pl.loop(0, chips)
     def _(i):
@@ -325,36 +293,57 @@
         for j in range(1, dps):
             cross(i, other(j), k).wait_send()
 
-    for j in range(1, dps):
-        kk = other(j)
-
-        @pl.loop(0, tiles)
-        def _(m):
-            up_send(j, m, kk, j - 1, kk).wait_recv()
-            up_send(j, m, kk, dps - 1 - j, k).wait_send()
-
     put_up.wait()
     put_down.wait()
-    put_in.wait()
-
-
-def hand_on(a, b, c, d, a_out, b_out, c_out, d_out, a_buf, b_buf, c_buf, d_buf, sems):
-    buffers = (a_buf, b_buf, c_buf, d_buf)
-    ins = [
-        pltpu.make_async_copy(ref, buf, sems.at[0, n])
-        for n, (ref, buf) in enumerate(zip((a, b, c, d), buffers))
+    put_own.wait()
+
+
+def one_hot(ids_ref, slots_ref, g, chips, rows):
+    place = ids_ref[...] * rows + slots_ref[...]
+    row = lax.broadcasted_iota(jnp.int32, (rows, place.shape[1]), 0)
+    blocks = [jnp.where(place - xor(g, p, chips) * rows == row, 1.0, 0.0) for p in range(chips)]
+    return jnp.concatenate(blocks, axis=0)
+
+
+def finish(
+    chips, cap, rows, ids_ref, slots_ref, gates_ref, fin, up_in, down_in,
+    in_hbm, gate_ref, up_out, down_out, fin_buf, up_buf, down_buf, in_buf, sems,
+):
+    g = lax.axis_index("expert") // 2
+    loads = [
+        pltpu.make_async_copy(src, buf, sems.at[0, n])
+        for n, (src, buf) in enumerate(((fin, fin_buf), (up_in, up_buf), (down_in, down_buf)))
     ]
-    outs = [
-        pltpu.make_async_copy(buf, ref, sems.at[1, n])
-        for n, (ref, buf) in enumerate(zip((a_out, b_out, c_out, d_out), buffers))
+    stores = [
+        pltpu.make_async_copy(buf, dst, sems.at[1, n])
+        for n, (buf, dst) in enumerate(((in_buf, in_hbm), (up_buf, up_out), (down_buf, down_out)))
     ]
-    for copy in ins:
-        copy.start()
-    for first, then in zip(ins, outs):
-        first.wait()
-        then.start()
-    for copy in outs:
-        copy.wait()
+    for load in loads:
+        load.start()
+    hot = one_hot(ids_ref, slots_ref, g, chips, rows)
+    hot16 = hot.astype(BF16)
+    for n in (1, 2):
+        loads[n].wait()
+        stores[n].start()
+    loads[0].wait()
+    half = fin_buf.shape[2]
+    back = fin_buf[...].astype(F32)
+    left = back[:, :rows].reshape(chips * rows, half).astype(BF16)
+    right = back[:, rows:].reshape(chips * rows, half).astype(BF16)
+    in_buf[:, :half] = dot(hot16, left, 0, 0).astype(BF16)
+    in_buf[:, half:] = dot(hot16, right, 0, 0).astype(BF16)
+    stores[0].start()
+    eye = lax.broadcasted_iota(jnp.int32, (1, rows, 128), 1) == lax.broadcasted_iota(
+        jnp.int32, (1, rows, 128), 2
+    )
+    col = jnp.sum(
+        jnp.where(eye, back[:, cap : cap + 1, :128], 0.0), axis=2, keepdims=True
+    ).reshape(chips * rows, 1)
+    scaled = jnp.sum(hot * col, axis=0, keepdims=True)
+    gates = gates_ref[...].astype(F32).reshape(1, -1)
+    gate_ref[...] = (scaled / gates).astype(BF16).reshape(gate_ref.shape)
+    for store in stores:
+        store.wait()
 
 
 def on_device(tokens_in, out_grad, gates, expert_ids, slot_ids, w_up, w_down):
@@ -368,69 +357,67 @@
     hq = hidden // dps
     dblk = width // dps
     slots = 2 * dps * chips * rows
-    tiles = dblk // min(256, dblk)
     vmem = pl.BlockSpec(memory_space=pltpu.VMEM)
     hbm = pl.BlockSpec(memory_space=pl.ANY)
     dma = pltpu.SemaphoreType.DMA
+    ids = expert_ids.reshape(1, tokens)
+    slot = slot_ids.reshape(1, tokens)
     raw = pl.pallas_call(
         functools.partial(kernel, chips, dps, cap, rows),
+        out_shape=(
+            jax.ShapeDtypeStruct((chips, 2 * rows, width // 2), BF16),
+            jax.ShapeDtypeStruct((dblk, hidden), BF16),
+            jax.ShapeDtypeStruct((hq, width), BF16),
+        ),
+        in_specs=[vmem] * 3 + [hbm] * 4,
+        out_specs=(hbm,) * 3,
+        scratch_shapes=[
+            pltpu.VMEM((tokens, width), BF16),
+            pltpu.VMEM((tokens, width), BF16),
+            pltpu.VMEM((dblk, hidden), BF16),
+            pltpu.VMEM((hq, width), BF16),
+            pltpu.VMEM((chips, 2 * rows - 8, width), BF16),
+            pltpu.VMEM((dps, chips, 2, 2 * rows - 8, width), BF16),
+            pltpu.VMEM((slots, width), BF16),
+            pltpu.VMEM((slots, width), BF16),
+            pltpu.VMEM((slots, hq), BF16),
+            pltpu.VMEM((slots, hidden), BF16),
+            pltpu.VMEM((4 * rows, hidden), BF16),
+            pltpu.VMEM((chips, 2, 2 * rows, width // 2), BF16),
+            pltpu.VMEM((chips, 2 * rows, width // 2), BF16),
+            pltpu.VMEM((width, hidden), BF16),
+            pltpu.VMEM((hidden, width), BF16),
+            dma((4,)),
+            dma((3,)),
+            dma((chips,)),
+            dma((chips,)),
+            dma((chips, dps)),
+            dma((chips, dps)),
+            dma((chips, dps)),
+            dma((chips, dps)),
+            dma((chips,)),
+            dma((chips,)),
+            dma((chips,)),
+            dma((chips,)),
+        ],
+        compiler_params=pltpu.CompilerParams(
+            collective_id=0, has_side_effects=True, vmem_limit_bytes=61 * 1024 * 1024
+        ),
+    )(ids, slot, gates, tokens_in, out_grad, w_up, w_down)
+    in_grad, gate_grad, up_grad, down_grad = pl.pallas_call(
+        functools.partial(finish, chips, cap, rows),
         out_shape=(
             jax.ShapeDtypeStruct((tokens, width), BF16),
             jax.ShapeDtypeStruct((tokens,), BF16),
             jax.ShapeDtypeStruct((dblk, hidden), BF16),
             jax.ShapeDtypeStruct((hq, width), BF16),
         ),
-        in_specs=[vmem] * 3 + [hbm] * 4,
+        in_specs=[vmem] * 3 + [hbm] * 3,
         out_specs=(hbm, vmem, hbm, hbm),
-        scratch_shapes=[
-            pltpu.VMEM((tokens, width), BF16),
-            pltpu.VMEM((tokens, width), BF16),
-            pltpu.VMEM((tokens, width), BF16),
-            pltpu.VMEM((dblk, hq), BF16),
-            pltpu.VMEM((hq, width), BF16),
-            pltpu.VMEM((chips, 2 * rows - 8, width), BF16),
-            pltpu.VMEM((dps, chips, 2, 2 * rows - 8, width), BF16),
-            pltpu.VMEM((slots, width), BF16),
-            pltpu.VMEM((slots, width), BF16),
-            pltpu.VMEM((slots, hq), BF16),
-            pltpu.VMEM((slots, hq), BF16),
-            pltpu.VMEM((4 * rows, hidden), BF16),
-            pltpu.VMEM((4 * rows, hidden), BF16),
-            pltpu.VMEM((chips, 2, 2 * rows, width // 2), BF16),
-            pltpu.VMEM((chips, 2 * rows, width // 2), BF16),
-            pltpu.VMEM((chips, 2 * rows, width // 2), BF16),
-            pltpu.VMEM((width, hidden), BF16),
-            pltpu.VMEM((hidden, width), BF16),
-            pltpu.VMEM((dps - 1, dblk, hq), BF16),
-            dma((4,)),
-            dma((3,)),
-            dma((chips,)),
-            dma((chips,)),
-            dma((chips, dps)),
-            dma((chips, dps)),
-            dma((chips, dps)),
-            dma((chips, dps)),
-            dma((chips,)),
-            dma((chips,)),
-            dma((chips,)),
-            dma((chips,)),
-            dma((dps, tiles)),
-            dma((dps, tiles)),
-        ],
-        compiler_params=pltpu.CompilerParams(
-            collective_id=0, has_side_effects=True, vmem_limit_bytes=61 * 1024 * 1024
-        ),
-    )(
-        expert_ids.reshape(1, tokens), slot_ids.reshape(1, tokens), gates,
-        tokens_in, out_grad, w_up, w_down,
-    )
-    in_grad, gate_grad, up_grad, down_grad = pl.pallas_call(
-        hand_on,
-        out_shape=[jax.ShapeDtypeStruct(r.shape, r.dtype) for r in raw],
-        in_specs=[hbm] * 4,
-        out_specs=[hbm] * 4,
-        scratch_shapes=[pltpu.VMEM(r.shape, r.dtype) for r in raw] + [dma((2, 4))],
-    )(*raw)
+        scratch_shapes=[pltpu.VMEM(r.shape, r.dtype) for r in raw]
+        + [pltpu.VMEM((tokens, width), BF16), dma((2, 3))],
+        compiler_params=pltpu.CompilerParams(vmem_limit_bytes=32 * 1024 * 1024),
+    )(ids, slot, gates, *raw)
     return (in_grad, gate_grad, up_grad[None], down_grad[None])
 
 

time: 62.5 us -> 57.5 us (0.920); the launches traced: 62.3 us -> 56.7 us
  Pallas kernels: 61.7 us -> 52.4 us
  local copies, waits for them, and re-layouts: 0 us -> 3.54 us
    pallas_call x1, Pallas kernels: 58.9 us -> 50 us  [on_device(): pl.pallas_call(functools.partial(kernel, chips, dps, cap, rows), out_shap...]
    unnamed x0 -> x12, local copies, waits for them, and re-layouts: none -> 3.54 us
where the time goes in v4:
time: 57.5 us; the launch traced here: 56.7 us
  Pallas kernels  52.4 us (91%)
  local copies, waits for them, and re-layouts  3.54 us (6%)
  between operations  0.7 us (1%)
    pallas_call x1, Pallas kernels, on_device(): pl.pallas_call(functools.partial(kernel, chips, dps, cap, rows), out_shap...  50 us
    unnamed x12, local copies, waits for them, and re-layouts  3.54 us
    pallas_call x1, Pallas kernels, on_device(): pl.pallas_call(functools.partial(finish, chips, cap, rows), out_shape=(ja...  2.44 us

profile of v4, /device:TPU:0, one launch (start us, length us, event | category | flops | bytes accessed | tf_op | source)
XLA Modules:
  0.0 56.7 jit_solution(13479880043998011768)
XLA Ops:
  0.6 0.0 copy-start.3
  0.6 0.0 copy-start.4
  0.7 0.0 copy-start.5
  0.7 50.0 %shard_map.102 = (bf16[8,80,512]{2,1,0:T(8,128)(2,1)}, bf16[512,1024]{1,0:T(8,128)(2,1)}, bf16[512,1024]{1,0:T(8,128)(2,1)}) custom-call(s32[1,256]{1,0:T(1,128)} %bitcast.4, s32[1,256]{1,0:T(1,128)} %bitcast.6, bf16[256]{0:T(256)(128)(2,1)} %gates_ref.3, bf16[256,1024]{1,0:T(8,128)(2,1)} %tok_hbm.1, bf16[256,1024]{1,0:T(8,128)(2,1)} %cot_hbm.1, ...), custom_call_target="tpu_custom_call" | custom-call | tf_op jit(solution)/shard_map/pallas_call | solution.py:365
  50.7 0.0 copy-done.3
  50.7 0.0 copy-done.4
  50.7 0.0 copy-done.5
  50.7 0.0 copy-start
  50.7 1.2 %copy-done = bf16[512,1024]{1,0:T(8,128)(2,1)S(1)} copy-done((bf16[512,1024]{1,0:T(8,128)(2,1)S(1)}, bf16[512,1024]{1,0:T(8,128)(2,1)}, u32[]{:S(2)}) %copy-start) | copy-done | bytes 1048600
  51.9 0.0 copy-start.1
  51.9 1.2 %copy-done.1 = bf16[512,1024]{1,0:T(8,128)(2,1)S(1)} copy-done((bf16[512,1024]{1,0:T(8,128)(2,1)S(1)}, bf16[512,1024]{1,0:T(8,128)(2,1)}, u32[]{:S(2)}) %copy-start.1) | copy-done | bytes 1048600
  53.1 0.0 copy-start.2
  53.1 1.1 %copy-done.2 = bf16[8,80,512]{2,1,0:T(8,128)(2,1)S(1)} copy-done((bf16[8,80,512]{2,1,0:T(8,128)(2,1)S(1)}, bf16[8,80,512]{2,1,0:T(8,128)(2,1)}, u32[]{:S(2)}) %copy-start.2) | copy-done | bytes 655384
  54.2 2.4 %shard_map.103 = (bf16[256,1024]{1,0:T(8,128)(2,1)}, bf16[256]{0:T(256)(128)(2,1)}, bf16[512,1024]{1,0:T(8,128)(2,1)}, bf16[512,1024]{1,0:T(8,128)(2,1)}) custom-call(s32[1,256]{1,0:T(1,128)S(1)} %bitcast.5, s32[1,256]{1,0:T(1,128)S(1)} %bitcast.7, bf16[256]{0:T(256)(128)(2,1)S(1)} %copy-done.5, bf16[8,80,512]{2,1,0:T(8,128)(2,1)S(1)} %copy-done.2, ...), custom_call_target="tpu_custom_call" | custom-call | tf_op jit(solution)/shard_map/pallas_call | solution.py:407
Async XLA Ops:
  0.6 50.0 %copy-start.3 = (s32[256]{0:T(256)S(1)}, s32[256]{0:T(256)}, u32[]{:S(2)}) copy-start(s32[256]{0:T(256)} %param.10) | copy-start | bytes 3076
  0.6 50.0 %copy-start.4 = (s32[256]{0:T(256)S(1)}, s32[256]{0:T(256)}, u32[]{:S(2)}) copy-start(s32[256]{0:T(256)} %param.11) | copy-start | bytes 3076
  0.7 50.0 %copy-start.5 = (bf16[256]{0:T(256)(128)(2,1)S(1)}, bf16[256]{0:T(256)(128)(2,1)}, u32[]{:S(2)}) copy-start(bf16[256]{0:T(256)(128)(2,1)} %gates_ref.3) | copy-start | bytes 1540
  50.7 1.2 %copy-start = (bf16[512,1024]{1,0:T(8,128)(2,1)S(1)}, bf16[512,1024]{1,0:T(8,128)(2,1)}, u32[]{:S(2)}) copy-start(bf16[512,1024]{1,0:T(8,128)(2,1)} %get-tuple-element.12.up_in) | copy-start | bytes 3145732
  51.9 1.2 %copy-start.1 = (bf16[512,1024]{1,0:T(8,128)(2,1)S(1)}, bf16[512,1024]{1,0:T(8,128)(2,1)}, u32[]{:S(2)}) copy-start(bf16[512,1024]{1,0:T(8,128)(2,1)} %get-tuple-element.13.down_in) | copy-start | bytes 3145732
  53.1 1.1 %copy-start.2 = (bf16[8,80,512]{2,1,0:T(8,128)(2,1)S(1)}, bf16[8,80,512]{2,1,0:T(8,128)(2,1)}, u32[]{:S(2)}) copy-start(bf16[8,80,512]{2,1,0:T(8,128)(2,1)} %get-tuple-element.11.fin) | copy-start | bytes 1966084

commit v5 on v4

--- a/solution.py
+++ b/solution.py
@@ -93,8 +93,6 @@
     load_down = pltpu.make_async_copy(down_hbm.at[0], wd, w_sem.at[1])
     load_tok.start()
     load_cot.start()
-    load_up.start()
-    load_down.start()
 
     barrier = pltpu.get_barrier_semaphore()
 
@@ -120,27 +118,37 @@
         flat = pltpu.roll(tiles8.reshape(count * 8, width), shift, 0)
         return flat.reshape(count, 8, width)
 
-    hot = one_hot(ids_ref, slots_ref, g, chips, rows)
-    hot16 = hot.astype(BF16)
+    def pack(first, hot):
+        count = hot.shape[0] // rows
+        hot16 = hot.astype(BF16)
+        gate_col = jnp.sum(hot * gates, axis=1, keepdims=True)
+        x = dot(hot16, tok_ref[...], 1, 0).reshape(count, rows, width)
+        d = (dot(hot16, cot_ref[...], 1, 0) * gate_col).reshape(count, rows, width)
+        mixed = jnp.where(upper, x[:, full:], rolled(d[:, full:], 4))
+        both = jnp.concatenate([x[:, :full], mixed, d[:, :full]], axis=1).astype(BF16)
+        tx[first : first + count] = both
+        if first == 0:
+            rx[k, 0, c] = both[0]
+
     gates = gates_ref[...].astype(F32).reshape(1, -1)
-    gate_col = jnp.sum(hot * gates, axis=1, keepdims=True)
+    near = one_hot(ids_ref, slots_ref, g, chips, rows, range(chips // 2))
+    far = one_hot(ids_ref, slots_ref, g, chips, rows, range(chips // 2, chips))
     load_tok.wait()
     load_cot.wait()
-    x_pack = dot(hot16, tok_ref[...], 1, 0).reshape(chips, rows, width)
-    d_pack = (dot(hot16, cot_ref[...], 1, 0) * gate_col).reshape(chips, rows, width)
-    mixed = jnp.where(upper, x_pack[:, full:], rolled(d_pack[:, full:], 4))
-    both = jnp.concatenate([x_pack[:, :full], mixed, d_pack[:, :full]], axis=1).astype(BF16)
-    tx[...] = both
-    rx[k, 0, c] = both[0]
-
+    load_up.start()
+    load_down.start()
+    pack(chips // 2, far)
     pl.semaphore_wait(barrier, chips - 1 + 1 + dps - 1)
 
-    ici(chips // 2).start()
+    @pl.loop(chips // 2, chips)
+    def _(i):
+        ici(i).start()
+
+    pack(0, near)
 
     @pl.loop(1, chips // 2)
     def _(i):
         ici(i).start()
-        ici(chips // 2 + i).start()
 
     def stage_a(i):
         @pl.when(i > 0)
@@ -298,10 +306,10 @@
     put_own.wait()
 
 
-def one_hot(ids_ref, slots_ref, g, chips, rows):
+def one_hot(ids_ref, slots_ref, g, chips, rows, positions):
     place = ids_ref[...] * rows + slots_ref[...]
     row = lax.broadcasted_iota(jnp.int32, (rows, place.shape[1]), 0)
-    blocks = [jnp.where(place - xor(g, p, chips) * rows == row, 1.0, 0.0) for p in range(chips)]
+    blocks = [jnp.where(place - xor(g, p, chips) * rows == row, 1.0, 0.0) for p in positions]
     return jnp.concatenate(blocks, axis=0)
 
 
@@ -320,7 +328,7 @@
     ]
     for load in loads:
         load.start()
-    hot = one_hot(ids_ref, slots_ref, g, chips, rows)
+    hot = one_hot(ids_ref, slots_ref, g, chips, rows, range(chips))
     hot16 = hot.astype(BF16)
     for n in (1, 2):
         loads[n].wait()
@@ -416,7 +424,7 @@
         out_specs=(hbm, vmem, hbm, hbm),
         scratch_shapes=[pltpu.VMEM(r.shape, r.dtype) for r in raw]
         + [pltpu.VMEM((tokens, width), BF16), dma((2, 3))],
-        compiler_params=pltpu.CompilerParams(vmem_limit_bytes=32 * 1024 * 1024),
+        compiler_params=pltpu.CompilerParams(vmem_limit_bytes=61 * 1024 * 1024),
     )(ids, slot, gates, *raw)
     return (in_grad, gate_grad, up_grad[None], down_grad[None])
 

time: 57.5 us -> 58 us (level)
  Pallas kernels: 52.4 us -> 57.1 us
  local copies, waits for them, and re-layouts: 3.54 us -> 0 us
    unnamed x12 -> x0, local copies, waits for them, and re-layouts: 3.54 us -> none
    pallas_call x1, Pallas kernels: 50 us -> 52.8 us  [on_device(): pl.pallas_call(functools.partial(kernel, chips, dps, cap, rows), out_shap...]
    pallas_call x1, Pallas kernels: 2.44 us -> 4.26 us  [on_device(): pl.pallas_call(functools.partial(finish, chips, cap, rows), out_shape=(ja...]
where the time goes in v5:
time: 58 us; the launch traced here: 57.7 us
  Pallas kernels  57.1 us (98%)
  between operations  0.64 us (1%)
    pallas_call x1, Pallas kernels, on_device(): pl.pallas_call(functools.partial(kernel, chips, dps, cap, rows), out_shap...  52.8 us
    pallas_call x1, Pallas kernels, on_device(): pl.pallas_call(functools.partial(finish, chips, cap, rows), out_shape=(ja...  4.26 us

profile of v5, /device:TPU:0, one launch (start us, length us, event | category | flops | bytes accessed | tf_op | source)
XLA Modules:
  0.0 57.7 jit_solution(12364395608419263789)
XLA Ops:
  0.6 52.8 %shard_map.102 = (bf16[8,80,512]{2,1,0:T(8,128)(2,1)}, bf16[512,1024]{1,0:T(8,128)(2,1)}, bf16[512,1024]{1,0:T(8,128)(2,1)}) custom-call(s32[1,256]{1,0:T(1,128)} %bitcast.4, s32[1,256]{1,0:T(1,128)} %bitcast.6, bf16[256]{0:T(256)(128)(2,1)} %gates_ref.3, bf16[256,1024]{1,0:T(8,128)(2,1)} %tok_hbm.1, bf16[256,1024]{1,0:T(8,128)(2,1)} %cot_hbm.1, ...), custom_call_target="tpu_custom_call" | custom-call | tf_op jit(solution)/shard_map/pallas_call | solution.py:373
  53.5 4.3 %shard_map.103 = (bf16[256,1024]{1,0:T(8,128)(2,1)}, bf16[256]{0:T(256)(128)(2,1)}, bf16[512,1024]{1,0:T(8,128)(2,1)}, bf16[512,1024]{1,0:T(8,128)(2,1)}) custom-call(s32[1,256]{1,0:T(1,128)} %bitcast.5, s32[1,256]{1,0:T(1,128)} %bitcast.7, bf16[256]{0:T(256)(128)(2,1)} %gates_ref.3, bf16[8,80,512]{2,1,0:T(8,128)(2,1)} %get-tuple-element.11.fin, ...), custom_call_target="tpu_custom_call" | custom-call | tf_op jit(solution)/shard_map/pallas_call | solution.py:415

commit v6 on v4

--- a/solution.py
+++ b/solution.py
@@ -362,6 +362,9 @@
     dma = pltpu.SemaphoreType.DMA
     ids = expert_ids.reshape(1, tokens)
     slot = slot_ids.reshape(1, tokens)
+    held = chips * 2 * rows * width * (1 + 2 * dps + 2 + 1) + slots * (2 * width + hq + hidden)
+    held += 2 * hidden * width + tokens * 2 * width + dblk * hidden + hq * width + 4 * rows * hidden
+    limit = (49 if 2 * held < 40 * 2**20 else 61) * 2**20
     raw = pl.pallas_call(
         functools.partial(kernel, chips, dps, cap, rows),
         out_shape=(
@@ -401,7 +404,7 @@
             dma((chips,)),
         ],
         compiler_params=pltpu.CompilerParams(
-            collective_id=0, has_side_effects=True, vmem_limit_bytes=61 * 1024 * 1024
+            collective_id=0, has_side_effects=True, vmem_limit_bytes=limit
         ),
     )(ids, slot, gates, tokens_in, out_grad, w_up, w_down)
     in_grad, gate_grad, up_grad, down_grad = pl.pallas_call(

time: 57.5 us -> 58.2 us (1.012)
  the two profiles are of different devices: /device:TPU:0 before, /device:TPU:16 now
where the time goes in v6:
time: 58.2 us; the launch traced here: 57.9 us
  Pallas kernels  53.2 us (91%)
  local copies, waits for them, and re-layouts  4.09 us (7%)
  between operations  0.65 us (1%)
    pallas_call x1, Pallas kernels, on_device(): pl.pallas_call(functools.partial(kernel, chips, dps, cap, rows), out_shap...  50.7 us
    unnamed x10, local copies, waits for them, and re-layouts  4.09 us
    pallas_call x1, Pallas kernels, on_device(): pl.pallas_call(functools.partial(finish, chips, cap, rows), out_shape=(ja...  2.46 us

profile of v6, /device:TPU:16, one launch (start us, length us, event | category | flops | bytes accessed | tf_op | source)
XLA Modules:
  0.0 57.9 jit_solution(49062247401008035)
XLA Ops:
  0.6 0.0 copy-start
  0.6 1.0 %copy-done = bf16[256,1024]{1,0:T(8,128)(2,1)S(1)} copy-done((bf16[256,1024]{1,0:T(8,128)(2,1)S(1)}, bf16[256,1024]{1,0:T(8,128)(2,1)}, u32[]{:S(2)}) %copy-start) | copy-done | bytes 524312
  1.7 0.0 copy-start.1
  1.7 1.0 %copy-done.1 = bf16[256,1024]{1,0:T(8,128)(2,1)S(1)} copy-done((bf16[256,1024]{1,0:T(8,128)(2,1)S(1)}, bf16[256,1024]{1,0:T(8,128)(2,1)}, u32[]{:S(2)}) %copy-start.1) | copy-done | bytes 524312
  2.7 0.0 copy-start.2
  2.7 0.7 %copy-done.2 = s32[256]{0:T(256)S(1)} copy-done((s32[256]{0:T(256)S(1)}, s32[256]{0:T(256)}, u32[]{:S(2)}) %copy-start.2) | copy-done | bytes 1048
  3.4 0.0 copy-start.3
  3.4 0.7 %copy-done.3 = s32[256]{0:T(256)S(1)} copy-done((s32[256]{0:T(256)S(1)}, s32[256]{0:T(256)}, u32[]{:S(2)}) %copy-start.3) | copy-done | bytes 1048
  4.1 0.0 copy-start.4
  4.1 0.7 %copy-done.4 = bf16[256]{0:T(256)(128)(2,1)S(1)} copy-done((bf16[256]{0:T(256)(128)(2,1)S(1)}, bf16[256]{0:T(256)(128)(2,1)}, u32[]{:S(2)}) %copy-start.4) | copy-done | bytes 536
  4.7 50.7 %shard_map.102 = (bf16[8,80,512]{2,1,0:T(8,128)(2,1)S(1)}, bf16[512,1024]{1,0:T(8,128)(2,1)S(1)}, bf16[512,1024]{1,0:T(8,128)(2,1)S(1)}) custom-call(s32[1,256]{1,0:T(1,128)S(1)} %bitcast.4, s32[1,256]{1,0:T(1,128)S(1)} %bitcast.6, bf16[256]{0:T(256)(128)(2,1)S(1)} %copy-done.4, bf16[256,1024]{1,0:T(8,128)(2,1)S(1)} %copy-done, ...), custom_call_target="tpu_custom_call" | custom-call | tf_op jit(solution)/shard_map/pallas_call | solution.py:368
  55.4 2.5 %shard_map.103 = (bf16[256,1024]{1,0:T(8,128)(2,1)}, bf16[256]{0:T(256)(128)(2,1)}, bf16[512,1024]{1,0:T(8,128)(2,1)}, bf16[512,1024]{1,0:T(8,128)(2,1)}) custom-call(s32[1,256]{1,0:T(1,128)S(1)} %bitcast.5, s32[1,256]{1,0:T(1,128)S(1)} %bitcast.7, bf16[256]{0:T(256)(128)(2,1)S(1)} %copy-done.4, bf16[8,80,512]{2,1,0:T(8,128)(2,1)S(1)} %get-tuple-element.11.fin, ...), custom_call_target="tpu_custom_call" | custom-call | tf_op jit(solution)/shard_map/pallas_call | solution.py:410
Async XLA Ops:
  0.6 1.0 %copy-start = (bf16[256,1024]{1,0:T(8,128)(2,1)S(1)}, bf16[256,1024]{1,0:T(8,128)(2,1)}, u32[]{:S(2)}) copy-start(bf16[256,1024]{1,0:T(8,128)(2,1)} %tok_hbm.1) | copy-start | bytes 1572868
  1.7 1.0 %copy-start.1 = (bf16[256,1024]{1,0:T(8,128)(2,1)S(1)}, bf16[256,1024]{1,0:T(8,128)(2,1)}, u32[]{:S(2)}) copy-start(bf16[256,1024]{1,0:T(8,128)(2,1)} %cot_hbm.1) | copy-start | bytes 1572868
  2.7 0.7 %copy-start.2 = (s32[256]{0:T(256)S(1)}, s32[256]{0:T(256)}, u32[]{:S(2)}) copy-start(s32[256]{0:T(256)} %param.10) | copy-start | bytes 3076
  3.4 0.7 %copy-start.3 = (s32[256]{0:T(256)S(1)}, s32[256]{0:T(256)}, u32[]{:S(2)}) copy-start(s32[256]{0:T(256)} %param.11) | copy-start | bytes 3076
  4.1 0.7 %copy-start.4 = (bf16[256]{0:T(256)(128)(2,1)S(1)}, bf16[256]{0:T(256)(128)(2,1)}, u32[]{:S(2)}) copy-start(bf16[256]{0:T(256)(128)(2,1)} %gates_ref.3) | copy-start | bytes 1540
